TPU v7x, 32 devices: a whole 2x2x4 slice. The times are simulated.
32 devices in a mesh: swath: 2 (over x), tile: 16 (over z, y, core).
Axes of the slice: x: 2, y: 2, z: 4, core: 2. Of those that a mesh axis runs over, the one named last changes fastest.
Arguments:
- traces: bfloat16 [1536, 768, 512], P(('swath', 'tile')), parts along dimension 0, may hold values from -6 to 6
- quality: int32 [1536, 768], P(('swath', 'tile')), parts along dimension 0, may hold values from 0 to 3
Outputs:
- multiples: bfloat16 [1536, 768, 512], P(('swath', 'tile')), parts along dimension 0
There are 2 independent parts, one for each index of `swath`. A program takes and returns all parts, laid end to end along the dimension named above; each array names one. Nothing has to cross between parts.
All inputs are finite; a program needn't handle non-finite values.
Results may differ from a plain program's by a relative error of at most 0.0077.
Values may be sent and summed in bfloat16 or wider, within the bound.
No kernel may reach another device: no remote copies, remote signals or barrier semaphores. Data moves between devices by JAX's collectives and lax.ppermute only.
A program may use at most 320 MiB of HBM per device.

v0:
```python
from functools import partial
import math

import jax
import jax.numpy as jnp
from jax import lax
from jax.sharding import PartitionSpec as P

NT = 512
NF = 64
F_LO = 8


def tables():
    bins = F_LO + jnp.arange(NF, dtype=jnp.int32)
    times = jnp.arange(NT, dtype=jnp.int32)
    phase = bins[:, None] * times[None, :] % NT
    angle = phase.astype(jnp.float32) * jnp.float32(2.0 * math.pi / NT)
    cosine = (jnp.cos(angle) / math.sqrt(NT)).astype(jnp.bfloat16)
    sine = (jnp.sin(angle) / math.sqrt(NT)).astype(jnp.bfloat16)
    return jnp.stack([cosine, -sine], axis=1)


def chain(pair, order):
    scale = 1.0 / math.sqrt(order)
    real_part = pair[0]
    imag_part = pair[1]
    scaled_real = real_part * scale
    scaled_imag = imag_part * scale
    operator_block = jnp.concatenate(
        [
            jnp.concatenate([scaled_real, scaled_imag], 1),
            jnp.concatenate([-scaled_imag, scaled_real], 1),
        ],
        0,
    )
    current = jnp.concatenate([real_part, imag_part], 1)
    first = jnp.dot(
        current, operator_block, precision=lax.Precision.HIGHEST, preferred_element_type=jnp.float32
    )
    second = jnp.dot(
        first, operator_block, precision=lax.Precision.HIGHEST, preferred_element_type=jnp.float32
    )
    third = jnp.dot(
        second, operator_block, precision=lax.Precision.HIGHEST, preferred_element_type=jnp.float32
    )
    predicted = first - second + third
    return jnp.stack([predicted[:, :order], predicted[:, order:]], 0)


def body(traces, quality):
    order = traces.shape[1]
    forward = tables()
    spectrum = lax.dot_general(
        forward, traces, (((2,), (2,)), ((), ())), preferred_element_type=jnp.float32
    )
    weight = (quality + 1).astype(jnp.float32)
    mirrored, mirror_weight = (
        lax.all_to_all(spectrum, "tile", split_axis=3, concat_axis=2, tiled=True),
        lax.all_to_all(weight[None, None], "tile", split_axis=3, concat_axis=2, tiled=True),
    )
    mirrored = jnp.swapaxes(mirrored, 2, 3)
    mirror_weight = mirror_weight[0, 0].T
    mixed = (weight * spectrum + mirror_weight * mirrored) / (weight + mirror_weight)
    blended = lax.all_to_all(mixed, "tile", split_axis=0, concat_axis=2, tiled=True)
    predicted = lax.map(partial(chain, order=order), blended)
    returned = lax.all_to_all(predicted, "tile", split_axis=2, concat_axis=0, tiled=True)
    inverse = forward.astype(jnp.float32)
    result = lax.dot_general(
        returned,
        inverse,
        (((0, 1), (0, 1)), ((), ())),
        precision=lax.Precision.HIGHEST,
        preferred_element_type=jnp.float32,
    )
    return result.astype(jnp.bfloat16)


def solution(mesh):
    in_specs = (P(("swath", "tile"), None, None), P(("swath", "tile"), None))
    out_specs = P(("swath", "tile"), None, None)
    return jax.shard_map(body, mesh=mesh, in_specs=in_specs, out_specs=out_specs, check_vma=False)
```

profile of v0, /device:TPU:15, one launch (start us, length us, event | category | flops | bytes accessed | tf_op | source)
XLA Modules:
  0.0 2040.2 jit_solution(10243115620339384655)
XLA Ops:
  0.0 0.9 add_convert_fusion
  0.9 0.3 copy.26
  1.3 0.5 broadcast.145
  1.7 1.5 reduce.1
  3.3 1.0 reshape.126
  4.3 6.6 all-to-all-start
  10.9 0.6 fusion.22
  11.5 0.6 multiply_convert_fusion.1
  12.1 0.6 copy-done.2
  12.7 22.4 %fusion.10 = f32[64,2,48,768]{3,0,2,1:T(8,128)} fusion(bf16[48,768,512]{2,1,0:T(8,128)(2,1)} %param.4, bf16[64,1,512]{2,0,1:T(8,128)(2,1)S(1)} %fusion.22, bf16[64,1,512]{2,0,1:T(8,128)(2,1)S(1)} %multiply_convert_fusion.1), kind=kOutput, calls=%fused_computation.21 | convolution fusion | flops 4832100352 | bytes 56754176 | tf_op jit(solution)/shard_map/dot_general | solution.py:54
  35.1 34.4 %copy.28 = f32[64,2,48,768]{0,2,1,3:T(8,128)} copy(f32[64,2,48,768]{3,0,2,1:T(8,128)} %fusion.10) | data formatting | bytes 37748736 | tf_op jit(solution)/shard_map/dot_general | solution.py:54
  69.5 31.3 %reshape.124 = f32[16,1,294912]{2,1,0:T(1,128)} reshape(f32[768,2,48,64]{3,2,1,0:T(8,128)} %bitcast.82) | data formatting | bytes 37748736
  100.8 6.7 all-to-all-start.1
  107.6 0.9 reduce.2
  108.5 0.8 reshape.127
  109.5 0.2 squeeze.11
  109.7 404.8 %all-to-all-done.1 = f32[16,1,294912]{2,1,0:T(1,128)} async-done(((f32[16,1,294912]{2,1,0:T(1,128)}), f32[16,1,294912]{2,1,0:T(1,128)}, u32[]{:S(2)}, u32[]{:S(2)}) %all-to-all-start.1) | async-done | bytes 18874400 | tf_op jit(solution)/shard_map/all_to_all | solution.py:59
  514.5 53.7 %reduce = f32[16,294912]{1,0:T(8,128)} reduce(f32[16,1,294912]{2,1,0:T(1,128)} %all-to-all-done.1, f32[]{:T(128)} %broadcast.145), dimensions={1}, to_apply=%all_to_all.53.reduce_sub_computation | reduce | bytes 37748740 | tf_op jit(solution)/shard_map/all_to_all | solution.py:59
  568.2 35.7 %reshape.125 = f32[768,2,48,64]{3,2,1,0:T(8,128)} reshape(f32[16,294912]{1,0:T(8,128)} %reduce) | data formatting | bytes 37748736
  604.0 45.4 %copy.40 = f32[64,2,16,48,48]{3,2,0,4,1:T(8,128)} copy(f32[64,2,16,48,48]{0,3,1,4,2:T(8,128)} %bitcast.83) | data formatting | bytes 37748736 | tf_op jit(solution)/shard_map/all_to_all | solution.py:59
  649.4 40.1 %reshape.123 = f32[64,2,768,48]{2,0,3,1:T(8,128)} reshape(f32[64,2,16,48,48]{3,2,0,4,1:T(8,128)} %copy.40) | data formatting | bytes 37748736 | tf_op jit(solution)/shard_map/all_to_all | solution.py:59
  689.4 13.0 fusion.13
  702.5 21.6 %copy.32 = f32[64,2,48,768]{3,2,1,0:T(8,128)} copy(f32[64,2,48,768]{3,0,2,1:T(8,128)S(1)} %fusion.13) | data formatting | bytes 37748736 | tf_op jit(solution)/shard_map/div | solution.py:64
  724.0 5.1 all-to-all-start.2
  729.2 406.8 %all-to-all-done.2 = f32[64,2,48,768]{3,2,1,0:T(8,128)} async-done(((f32[64,2,48,768]{3,2,1,0:T(8,128)}), f32[64,2,48,768]{3,2,1,0:T(8,128)}, u32[]{:S(2)}, u32[]{:S(2)}) %all-to-all-start.2) | async-done | bytes 18874400 | tf_op jit(solution)/shard_map/all_to_all | solution.py:65
  1136.0 12.7 copy.33
  1148.6 401.8 %while.10 = (s32[]{:T(128)}, f32[4,2,768,768]{3,1,0,2:T(2,128)}, f32[4,2,768,768]{3,2,1,0:T(8,128)}, s32[]{:T(128)}, s32[]{:T(128)}, /*index=5*/s32[]{}) while((s32[]{:T(128)}, f32[4,2,768,768]{3,1,0,2:T(2,128)}, f32[4,2,768,768]{3,2,1,0:T(8,128)}, s32[]{:T(128)}, s32[]{:T(128)}, /*index=5*/s32[]{}) %tuple.31), condition=%wide.region_1.2_spmd, body=%wide.region_0.1_spmd.sunk | while | flops 65258127360 | bytes 101450328 | solution.py:66
  1172.4 3.0 broadcast_multiply_fusion.3
  1175.4 0.2 fusion.43
  1175.6 28.2 %fusion.44 = f32[768,1536]{1,0:T(8,128)} fusion(f32[768,768]{1,0:T(8,128)S(1)} %get-tuple-element.64, f32[768,768]{1,0:T(8,128)S(1)} %get-tuple-element.65, f32[768,768]{1,0:T(8,128)S(1)} %get-tuple-element.66, f32[768,768]{1,0:T(8,128)S(1)} %fusion.43, f32[768,768]{1,0:T(8,128)S(1)} %get-tuple-element.67), kind=kOutput, calls=%fused_computation.1.clone.1 | convolution fusion | flops 21751529472 | bytes 16515072 | tf_op jit(solution)/shard_map/while/body/eval_jaxpr/dot_general | solution.py:38
  1203.8 26.3 %fusion.45 = f32[768,1536]{1,0:T(8,128)} fusion(f32[768,1536]{1,0:T(8,128)} %fusion.44, f32[768,768]{1,0:T(8,128)S(1)} %get-tuple-element.66, f32[768,768]{1,0:T(8,128)S(1)} %fusion.43, f32[768,768]{1,0:T(8,128)S(1)} %get-tuple-element.67), kind=kOutput, calls=%fused_computation.9.clone.1 | convolution fusion | flops 21750349824 | bytes 16515072 | tf_op jit(solution)/shard_map/while/body/eval_jaxpr/dot_general | solution.py:41
  1230.1 28.5 %subtract_add_fusion.2 = f32[768,1536]{1,0:T(8,128)S(1)} fusion(f32[768,1536]{1,0:T(8,128)} %fusion.44, f32[768,1536]{1,0:T(8,128)} %fusion.45, f32[768,768]{1,0:T(8,128)S(1)} %get-tuple-element.66, f32[768,768]{1,0:T(8,128)S(1)} %fusion.43, f32[768,768]{1,0:T(8,128)S(1)} %get-tuple-element.67), kind=kOutput, calls=%fused_computation.7.clone.1 | convolution fusion | flops 21752709120 | bytes 21233664 | tf_op jit(solution)/shard_map/while/body/eval_jaxpr/dot_general | solution.py:44
  1258.6 0.3 slice_bitcast_fusion.3
  1258.9 0.3 maximum_bitcast_fusion.2
  1259.2 5.8 copy_dynamic-update-slice_fusion.2
  1265.0 3.0 broadcast_multiply_fusion.3
  1268.0 0.2 fusion.43
  1268.2 28.2 %fusion.44 = f32[768,1536]{1,0:T(8,128)} fusion(f32[768,768]{1,0:T(8,128)S(1)} %get-tuple-element.64, f32[768,768]{1,0:T(8,128)S(1)} %get-tuple-element.65, f32[768,768]{1,0:T(8,128)S(1)} %get-tuple-element.66, f32[768,768]{1,0:T(8,128)S(1)} %fusion.43, f32[768,768]{1,0:T(8,128)S(1)} %get-tuple-element.67), kind=kOutput, calls=%fused_computation.1.clone.1 | convolution fusion | flops 21751529472 | bytes 16515072 | tf_op jit(solution)/shard_map/while/body/eval_jaxpr/dot_general | solution.py:38
  1296.4 26.3 %fusion.45 = f32[768,1536]{1,0:T(8,128)} fusion(f32[768,1536]{1,0:T(8,128)} %fusion.44, f32[768,768]{1,0:T(8,128)S(1)} %get-tuple-element.66, f32[768,768]{1,0:T(8,128)S(1)} %fusion.43, f32[768,768]{1,0:T(8,128)S(1)} %get-tuple-element.67), kind=kOutput, calls=%fused_computation.9.clone.1 | convolution fusion | flops 21750349824 | bytes 16515072 | tf_op jit(solution)/shard_map/while/body/eval_jaxpr/dot_general | solution.py:41
  1322.7 28.5 %subtract_add_fusion.2 = f32[768,1536]{1,0:T(8,128)S(1)} fusion(f32[768,1536]{1,0:T(8,128)} %fusion.44, f32[768,1536]{1,0:T(8,128)} %fusion.45, f32[768,768]{1,0:T(8,128)S(1)} %get-tuple-element.66, f32[768,768]{1,0:T(8,128)S(1)} %fusion.43, f32[768,768]{1,0:T(8,128)S(1)} %get-tuple-element.67), kind=kOutput, calls=%fused_computation.7.clone.1 | convolution fusion | flops 21752709120 | bytes 21233664 | tf_op jit(solution)/shard_map/while/body/eval_jaxpr/dot_general | solution.py:44
  1351.2 0.3 slice_bitcast_fusion.3
  1351.5 0.3 maximum_bitcast_fusion.2
  1351.8 5.8 copy_dynamic-update-slice_fusion.2
  1357.7 3.0 broadcast_multiply_fusion.3
  1360.7 0.2 fusion.43
  1360.9 28.2 %fusion.44 = f32[768,1536]{1,0:T(8,128)} fusion(f32[768,768]{1,0:T(8,128)S(1)} %get-tuple-element.64, f32[768,768]{1,0:T(8,128)S(1)} %get-tuple-element.65, f32[768,768]{1,0:T(8,128)S(1)} %get-tuple-element.66, f32[768,768]{1,0:T(8,128)S(1)} %fusion.43, f32[768,768]{1,0:T(8,128)S(1)} %get-tuple-element.67), kind=kOutput, calls=%fused_computation.1.clone.1 | convolution fusion | flops 21751529472 | bytes 16515072 | tf_op jit(solution)/shard_map/while/body/eval_jaxpr/dot_general | solution.py:38
  1389.1 26.3 %fusion.45 = f32[768,1536]{1,0:T(8,128)} fusion(f32[768,1536]{1,0:T(8,128)} %fusion.44, f32[768,768]{1,0:T(8,128)S(1)} %get-tuple-element.66, f32[768,768]{1,0:T(8,128)S(1)} %fusion.43, f32[768,768]{1,0:T(8,128)S(1)} %get-tuple-element.67), kind=kOutput, calls=%fused_computation.9.clone.1 | convolution fusion | flops 21750349824 | bytes 16515072 | tf_op jit(solution)/shard_map/while/body/eval_jaxpr/dot_general | solution.py:41
  1415.3 28.5 %subtract_add_fusion.2 = f32[768,1536]{1,0:T(8,128)S(1)} fusion(f32[768,1536]{1,0:T(8,128)} %fusion.44, f32[768,1536]{1,0:T(8,128)} %fusion.45, f32[768,768]{1,0:T(8,128)S(1)} %get-tuple-element.66, f32[768,768]{1,0:T(8,128)S(1)} %fusion.43, f32[768,768]{1,0:T(8,128)S(1)} %get-tuple-element.67), kind=kOutput, calls=%fused_computation.7.clone.1 | convolution fusion | flops 21752709120 | bytes 21233664 | tf_op jit(solution)/shard_map/while/body/eval_jaxpr/dot_general | solution.py:44
  1443.9 0.3 slice_bitcast_fusion.3
  1444.2 0.3 maximum_bitcast_fusion.2
  1444.5 5.8 copy_dynamic-update-slice_fusion.2
  1450.3 3.0 broadcast_multiply_fusion.3
  1453.3 0.2 fusion.43
  1453.5 28.2 %fusion.44 = f32[768,1536]{1,0:T(8,128)} fusion(f32[768,768]{1,0:T(8,128)S(1)} %get-tuple-element.64, f32[768,768]{1,0:T(8,128)S(1)} %get-tuple-element.65, f32[768,768]{1,0:T(8,128)S(1)} %get-tuple-element.66, f32[768,768]{1,0:T(8,128)S(1)} %fusion.43, f32[768,768]{1,0:T(8,128)S(1)} %get-tuple-element.67), kind=kOutput, calls=%fused_computation.1.clone.1 | convolution fusion | flops 21751529472 | bytes 16515072 | tf_op jit(solution)/shard_map/while/body/eval_jaxpr/dot_general | solution.py:38
  1481.7 26.3 %fusion.45 = f32[768,1536]{1,0:T(8,128)} fusion(f32[768,1536]{1,0:T(8,128)} %fusion.44, f32[768,768]{1,0:T(8,128)S(1)} %get-tuple-element.66, f32[768,768]{1,0:T(8,128)S(1)} %fusion.43, f32[768,768]{1,0:T(8,128)S(1)} %get-tuple-element.67), kind=kOutput, calls=%fused_computation.9.clone.1 | convolution fusion | flops 21750349824 | bytes 16515072 | tf_op jit(solution)/shard_map/while/body/eval_jaxpr/dot_general | solution.py:41
  1508.0 28.5 %subtract_add_fusion.2 = f32[768,1536]{1,0:T(8,128)S(1)} fusion(f32[768,1536]{1,0:T(8,128)} %fusion.44, f32[768,1536]{1,0:T(8,128)} %fusion.45, f32[768,768]{1,0:T(8,128)S(1)} %get-tuple-element.66, f32[768,768]{1,0:T(8,128)S(1)} %fusion.43, f32[768,768]{1,0:T(8,128)S(1)} %get-tuple-element.67), kind=kOutput, calls=%fused_computation.7.clone.1 | convolution fusion | flops 21752709120 | bytes 21233664 | tf_op jit(solution)/shard_map/while/body/eval_jaxpr/dot_general | solution.py:44
  1536.5 0.3 slice_bitcast_fusion.3
  1536.8 0.3 maximum_bitcast_fusion.2
  1537.1 5.8 copy_dynamic-update-slice_fusion.2
  1550.4 5.4 all-to-all-start.3
  1555.9 406.7 %all-to-all-done.3 = f32[4,2,768,768]{3,1,0,2:T(2,128)} async-done(((f32[4,2,768,768]{3,1,0,2:T(2,128)}), f32[4,2,768,768]{3,1,0,2:T(2,128)}, u32[]{:S(2)}, u32[]{:S(2)}) %all-to-all-start.3) | async-done | bytes 18874400 | tf_op jit(solution)/shard_map/all_to_all | solution.py:67
  1962.5 19.3 copy.47
  1981.8 21.9 %all_to_all.64 = f32[64,2,48,768]{3,0,1,2:T(8,128)} reshape(f32[16,4,2,48,768]{4,1,0,2,3:T(4,128)} %bitcast.85) | data formatting | bytes 37748736 | tf_op jit(solution)/shard_map/all_to_all | solution.py:67
  2003.8 36.2 %bitcast_convert_fusion = bf16[48,768,512]{2,1,0:T(8,128)(2,1)} fusion(f32[64,2,48,768]{3,0,1,2:T(8,128)} %all_to_all.64, bf16[64,2,512,1]{2,0,1,3:T(8,128)(2,1)S(1)} %fusion.32), kind=kOutput, calls=%fused_computation.20 | convolution fusion | flops 29009903616 | bytes 56754176 | tf_op jit(solution)/shard_map/dot_general | solution.py:69
  (15 shorter events, 0.2 us)
Async XLA Ops:
  4.3 96.5 %all-to-all-start = ((f32[16,1,2304]{2,1,0:T(1,128)}), f32[16,1,2304]{2,1,0:T(1,128)S(1)}, u32[]{:S(2)}, u32[]{:S(2)}) async-start(f32[16,1,2304]{2,1,0:T(1,128)} %reshape.126), calls=%async_computation | async-start | bytes 294912 | tf_op jit(solution)/shard_map/all_to_all | solution.py:60
  11.5 0.6 copy-start
  12.1 0.6 copy-start.2
  100.8 8.8 copy-start.4
  100.8 413.7 %all-to-all-start.1 = ((f32[16,1,294912]{2,1,0:T(1,128)}), f32[16,1,294912]{2,1,0:T(1,128)}, u32[]{:S(2)}, u32[]{:S(2)}) async-start(f32[16,1,294912]{2,1,0:T(1,128)} %reshape.124), calls=%async_computation.1 | async-start | bytes 37748736 | tf_op jit(solution)/shard_map/all_to_all | solution.py:59
  724.0 411.9 %all-to-all-start.2 = ((f32[64,2,48,768]{3,2,1,0:T(8,128)}), f32[64,2,48,768]{3,2,1,0:T(8,128)}, u32[]{:S(2)}, u32[]{:S(2)}) async-start(f32[64,2,48,768]{3,2,1,0:T(8,128)} %copy.32), calls=%async_computation.2 | async-start | bytes 37748736 | tf_op jit(solution)/shard_map/all_to_all | solution.py:65
  1550.4 5.4 copy-start.1
  1550.4 5.4 copy-start.3
  1550.4 412.1 %all-to-all-start.3 = ((f32[4,2,768,768]{3,1,0,2:T(2,128)}), f32[4,2,768,768]{3,1,0,2:T(2,128)}, u32[]{:S(2)}, u32[]{:S(2)}) async-start(f32[4,2,768,768]{3,1,0,2:T(2,128)} %get-tuple-element.22), calls=%async_computation.3 | async-start | bytes 37748736 | tf_op jit(solution)/shard_map/all_to_all | solution.py:67
where the time goes:
time: 2050 us; the launch traced here: 2040 us
  waiting for transfers between devices  1220 us (60%)
  matrix products  391 us (19%)
  local copies, waits for them, and re-layouts  291 us (14%)
  other arithmetic  85.2 us (4%)
  loops' own time  31.4 us (2%)
  starting transfers between devices  23.8 us (1%)
    all_to_all x1, waiting for transfers between devices, body(): lax.all_to_all(mixed, 'tile', split_axis=0, concat_axis=2, tiled=True)  407 us
    all_to_all x1, waiting for transfers between devices, body(): lax.all_to_all(predicted, 'tile', split_axis=2, concat_axis=0, tiled=True)  407 us
    all_to_all x1, waiting for transfers between devices, body(): lax.all_to_all(spectrum, 'tile', split_axis=3, concat_axis=2, tiled=True)  405 us
    dot_general x4, matrix products, chain(): jnp.dot(second, operator_block, precision=lax.Precision.HIGHEST, preferre...  114 us
    dot_general x4, matrix products, chain(): jnp.dot(current, operator_block, precision=lax.Precision.HIGHEST, preferr...  113 us
    dot_general x4, matrix products, chain(): jnp.dot(first, operator_block, precision=lax.Precision.HIGHEST, preferred...  105 us
    all_to_all x3, local copies, waits for them, and re-layouts, body(): lax.all_to_all(spectrum, 'tile', split_axis=3, concat_axis=2, tiled=True)  86 us
    unnamed x14, local copies, waits for them, and re-layouts  69.7 us
  transfers between devices with their start and end apart: 4, of which 3 were waited for; matrix products, arithmetic and copies ran while one was open for 4% of the time, Pallas kernels for 0%

commit v1 on v0

v1 whole, which is shorter than its diff:
```python
import math

import jax
import jax.numpy as jnp
from jax import lax
from jax.sharding import PartitionSpec as P

NT = 512
NF = 64
F_LO = 8


def tables():
    bins = F_LO + jnp.arange(NF, dtype=jnp.int32)
    times = jnp.arange(NT, dtype=jnp.int32)
    phase = bins[:, None] * times[None, :] % NT
    angle = phase.astype(jnp.float32) * jnp.float32(2.0 * math.pi / NT)
    cosine = (jnp.cos(angle) / math.sqrt(NT)).astype(jnp.bfloat16)
    sine = (jnp.sin(angle) / math.sqrt(NT)).astype(jnp.bfloat16)
    return jnp.stack([cosine, -sine], axis=1)


def mm(a, b):
    return jnp.dot(a, b, preferred_element_type=jnp.float32)


def cmul(ar, ai, br, bi):
    return mm(ar, br) - mm(ai, bi), mm(ar, bi) + mm(ai, br)


def chain(yr, yi):
    order = yr.shape[0]
    inv = 1.0 / math.sqrt(order)
    br = yr.astype(jnp.float32) + yr.T.astype(jnp.float32)
    bi = yi.astype(jnp.float32) + yi.T.astype(jnp.float32)
    b16r, b16i = br.astype(jnp.bfloat16), bi.astype(jnp.bfloat16)
    fr, fi = cmul(b16r, b16i, b16r, b16i)
    fr, fi = fr * inv, fi * inv
    gr, gi = (fr - br).astype(jnp.bfloat16), (fi - bi).astype(jnp.bfloat16)
    tr, ti = cmul(fr.astype(jnp.bfloat16), fi.astype(jnp.bfloat16), gr, gi)
    pr, pi = fr + tr * inv, fi + ti * inv
    return pr.astype(jnp.bfloat16), pi.astype(jnp.bfloat16)


def body(traces, quality):
    rows, order = quality.shape
    n = order // rows
    forward = tables()
    weight = (quality + 1).astype(jnp.float32)
    mirror = lax.all_to_all(
        weight.astype(jnp.bfloat16), "tile", split_axis=1, concat_axis=0, tiled=True
    )
    share = weight / (weight + mirror.T.astype(jnp.float32))
    returned = []
    for chunk in range(NF // n):
        part = forward[chunk * n : (chunk + 1) * n]
        spectrum = lax.dot_general(
            part, traces, (((2,), (2,)), ((), ())), preferred_element_type=jnp.float32
        )
        mixed = (share * spectrum).astype(jnp.bfloat16)
        got = lax.all_to_all(mixed, "tile", split_axis=0, concat_axis=0, tiled=True)
        pr, pi = chain(got[:, 0].reshape(order, order), got[:, 1].reshape(order, order))
        back = jnp.stack([pr.reshape(n, rows, order), pi.reshape(n, rows, order)], 1)
        returned.append(
            lax.all_to_all(back, "tile", split_axis=0, concat_axis=0, tiled=True)
        )
    result = lax.dot_general(
        jnp.concatenate(returned, 0),
        forward,
        (((0, 1), (0, 1)), ((), ())),
        preferred_element_type=jnp.float32,
    )
    return result.astype(jnp.bfloat16)


def solution(mesh):
    in_specs = (P(("swath", "tile"), None, None), P(("swath", "tile"), None))
    out_specs = P(("swath", "tile"), None, None)
    return jax.shard_map(body, mesh=mesh, in_specs=in_specs, out_specs=out_specs, check_vma=False)
```

time: 2050 us -> 533 us (0.26)
  waiting for transfers between devices: 1220 us -> 191 us
  matrix products: 391 us -> 136 us
  local copies, waits for them, and re-layouts: 291 us -> 94.6 us
  other arithmetic: 85.2 us -> 51.5 us
  loops' own time: 31.4 us -> 0 us
  starting transfers between devices: 23.8 us -> 49.6 us
    all_to_all x4 -> x9, waiting for transfers between devices: 1220 us -> 191 us  [the longest x4 95.4 us: body(): got = lax.all_to_all(mixed, 'tile', split_axis=0, concat_axis=0, tiled=True)]
    dot_general x14 -> x37, matrix products: 391 us -> 136 us  [the longest x4 71.1 us: body(): lax.dot_general(part, traces, (((2,), (2,)), ((), ())), preferred_element...]
    all_to_all x7 -> x5, local copies, waits for them, and re-layouts: 140 us -> 20.9 us  [the longest x4 20.8 us: body(): lax.all_to_all(back, 'tile', split_axis=0, concat_axis=0, tiled=True)]
    unnamed x14 -> x74, local copies, waits for them, and re-layouts: 69.7 us -> 11.1 us
    all_to_all x2 -> x0, other arithmetic: 54.6 us -> none  [the longest x1 53.7 us: body(): lax.all_to_all(spectrum, 'tile', split_axis=3, concat_axis=2, tiled=True)]
    dot_general x1 -> x0, local copies, waits for them, and re-layouts: 34.4 us -> none  [body(): lax.dot_general(forward, traces, (((2,), (2,)), ((), ())), preferred_elem...]
    another operation x1 -> x0, loops' own time: 31.4 us -> none  [body(): predicted = lax.map(partial(chain, order=order), blended)]
    another operation x0 -> x4, other arithmetic: none -> 29.6 us  [body(): jnp.stack([pr.reshape(n, rows, order), pi.reshape(n, rows, order)], 1)]
  transfers between devices with their start and end apart: 4 -> 9, of which waited for: 3 -> 9; matrix products, arithmetic and copies ran while one was open for 4% -> 43% of each run, Pallas kernels for 0% -> 0%
where the time goes in v1:
time: 533 us; the launch traced here: 524 us
  waiting for transfers between devices  191 us (36%)
  matrix products  136 us (26%)
  local copies, waits for them, and re-layouts  94.6 us (18%)
  other arithmetic  51.5 us (10%)
  starting transfers between devices  49.6 us (9%)
    all_to_all x4, waiting for transfers between devices, body(): got = lax.all_to_all(mixed, 'tile', split_axis=0, concat_axis=0, tiled=True)  95.4 us
    all_to_all x4, waiting for transfers between devices, body(): lax.all_to_all(back, 'tile', split_axis=0, concat_axis=0, tiled=True)  92.9 us
    dot_general x4, matrix products, body(): lax.dot_general(part, traces, (((2,), (2,)), ((), ())), preferred_element...  71.1 us
    dot_general x32, matrix products, mm(): return jnp.dot(a, b, preferred_element_type=jnp.float32)  46 us
    another operation x4, other arithmetic, body(): jnp.stack([pr.reshape(n, rows, order), pi.reshape(n, rows, order)], 1)  29.6 us
    another operation x8, local copies, waits for them, and re-layouts, body(): jnp.stack([pr.reshape(n, rows, order), pi.reshape(n, rows, order)], 1)  26.4 us
    all_to_all x4, starting transfers between devices, body(): got = lax.all_to_all(mixed, 'tile', split_axis=0, concat_axis=0, tiled=True)  22.8 us
    all_to_all x4, local copies, waits for them, and re-layouts, body(): lax.all_to_all(back, 'tile', split_axis=0, concat_axis=0, tiled=True)  20.8 us
  transfers between devices with their start and end apart: 9, of which 9 were waited for; matrix products, arithmetic and copies ran while one was open for 43% of the time, Pallas kernels for 0%

profile of v1, /device:TPU:15, one launch (start us, length us, event | category | flops | bytes accessed | tf_op | source)
XLA Modules:
  0.0 523.8 jit_solution(3030627289757421180)
XLA Ops:
  2.1 6.6 %all-to-all-start = ((bf16[16,2,1152]{2,1,0:T(2,128)(2,1)}), bf16[16,2,1152]{2,1,0:T(2,128)(2,1)S(1)}, u32[]{:S(2)}, u32[]{:S(2)}) async-start(bf16[16,2,1152]{2,1,0:T(2,128)(2,1)} %reshape.174), calls=%async_computation | async-start | bytes 147456 | tf_op jit(solution)/shard_map/all_to_all | solution.py:50
  9.8 3.2 all-to-all-done
  13.6 17.8 %multiply_convert_fusion.2 = bf16[16,2,48,768]{3,0,2,1:T(8,128)(2,1)S(1)} fusion(bf16[48,768,512]{2,1,0:T(8,128)(2,1)} %param.2, f32[48,768]{1,0:T(8,128)S(1)} %add_divide_fusion, bf16[64,1,512]{2,0,1:T(8,128)(2,1)S(1)} %multiply_convert_fusion.5, bf16[64,1,512]{2,0,1:T(8,128)(2,1)S(1)} %fusion.63), kind=kOutput, calls=%fused_computation.18 | convolution fusion | flops 1210384384 | bytes 40386560 | tf_op jit(solution)/shard_map/dot_general | solution.py:57
  31.4 2.1 copy.87
  33.5 7.0 %all-to-all-start.3 = ((bf16[16,2,48,768]{3,2,1,0:T(8,128)(2,1)}), bf16[16,2,48,768]{3,2,1,0:T(8,128)(2,1)}, u32[]{:S(2)}, u32[]{:S(2)}) async-start(bf16[16,2,48,768]{3,2,1,0:T(8,128)(2,1)} %copy.87), calls=%async_computation.3 | async-start | bytes 4718592 | tf_op jit(solution)/shard_map/all_to_all | solution.py:61
  40.5 17.8 %multiply_convert_fusion.3 = bf16[16,2,48,768]{3,0,2,1:T(8,128)(2,1)S(1)} fusion(bf16[48,768,512]{2,1,0:T(8,128)(2,1)} %param.2, f32[48,768]{1,0:T(8,128)S(1)} %add_divide_fusion, bf16[64,1,512]{2,0,1:T(8,128)(2,1)S(1)} %multiply_convert_fusion.5, bf16[64,1,512]{2,0,1:T(8,128)(2,1)S(1)} %fusion.63), kind=kOutput, calls=%fused_computation.19 | convolution fusion | flops 1210384384 | bytes 40386560 | tf_op jit(solution)/shard_map/dot_general | solution.py:57
  58.3 2.2 copy.80
  60.5 33.2 %all-to-all-done.3 = bf16[16,2,48,768]{3,2,1,0:T(8,128)(2,1)} async-done(((bf16[16,2,48,768]{3,2,1,0:T(8,128)(2,1)}), bf16[16,2,48,768]{3,2,1,0:T(8,128)(2,1)}, u32[]{:S(2)}, u32[]{:S(2)}) %all-to-all-start.3) | async-done | bytes 2359328 | tf_op jit(solution)/shard_map/all_to_all | solution.py:61
  93.7 4.9 all-to-all-start.1
  98.6 17.8 %multiply_convert_fusion = bf16[16,2,48,768]{3,0,2,1:T(8,128)(2,1)S(1)} fusion(bf16[48,768,512]{2,1,0:T(8,128)(2,1)} %param.2, f32[48,768]{1,0:T(8,128)S(1)} %add_divide_fusion, bf16[64,1,512]{2,0,1:T(8,128)(2,1)S(1)} %multiply_convert_fusion.5, bf16[64,1,512]{2,0,1:T(8,128)(2,1)S(1)} %fusion.63), kind=kOutput, calls=%fused_computation.16 | convolution fusion | flops 1210384384 | bytes 40386560 | tf_op jit(solution)/shard_map/dot_general | solution.py:57
  116.3 2.1 copy.101
  118.5 33.2 %all-to-all-done.1 = bf16[16,2,48,768]{3,2,1,0:T(8,128)(2,1)} async-done(((bf16[16,2,48,768]{3,2,1,0:T(8,128)(2,1)}), bf16[16,2,48,768]{3,2,1,0:T(8,128)(2,1)}, u32[]{:S(2)}, u32[]{:S(2)}) %all-to-all-start.1) | async-done | bytes 2359328 | tf_op jit(solution)/shard_map/all_to_all | solution.py:61
  151.7 5.3 %all-to-all-start.7 = ((bf16[16,2,48,768]{3,2,1,0:T(8,128)(2,1)}), bf16[16,2,48,768]{3,2,1,0:T(8,128)(2,1)}, u32[]{:S(2)}, u32[]{:S(2)}) async-start(bf16[16,2,48,768]{3,2,1,0:T(8,128)(2,1)} %copy.101), calls=%async_computation.7 | async-start | bytes 4718592 | tf_op jit(solution)/shard_map/all_to_all | solution.py:61
  157.1 17.8 %multiply_convert_fusion.1 = bf16[16,2,48,768]{3,0,2,1:T(8,128)(2,1)S(1)} fusion(bf16[48,768,512]{2,1,0:T(8,128)(2,1)} %param.2, f32[48,768]{1,0:T(8,128)S(1)} %add_divide_fusion, bf16[64,1,512]{2,0,1:T(8,128)(2,1)S(1)} %multiply_convert_fusion.5, bf16[64,1,512]{2,0,1:T(8,128)(2,1)S(1)} %fusion.63), kind=kOutput, calls=%fused_computation.17 | convolution fusion | flops 1210384384 | bytes 40386560 | tf_op jit(solution)/shard_map/dot_general | solution.py:57
  174.8 2.2 copy.94
  178.8 1.9 bitcast_convert_fusion.7
  180.7 2.0 copy.84
  182.7 2.0 copy.82
  184.8 2.2 fusion.24
  190.4 3.1 subtract_convert_fusion.6
  193.4 3.1 subtract_convert_fusion.7
  196.6 13.5 %all-to-all-done.7 = bf16[16,2,48,768]{3,2,1,0:T(8,128)(2,1)} async-done(((bf16[16,2,48,768]{3,2,1,0:T(8,128)(2,1)}), bf16[16,2,48,768]{3,2,1,0:T(8,128)(2,1)}, u32[]{:S(2)}, u32[]{:S(2)}) %all-to-all-start.7) | async-done | bytes 2359328 | tf_op jit(solution)/shard_map/all_to_all | solution.py:61
  210.1 5.6 %all-to-all-start.5 = ((bf16[16,2,48,768]{3,2,1,0:T(8,128)(2,1)}), bf16[16,2,48,768]{3,2,1,0:T(8,128)(2,1)}, u32[]{:S(2)}, u32[]{:S(2)}) async-start(bf16[16,2,48,768]{3,2,1,0:T(8,128)(2,1)} %copy.94), calls=%async_computation.5 | async-start | bytes 4718592 | tf_op jit(solution)/shard_map/all_to_all | solution.py:61
  218.8 3.6 copy.85
  224.6 3.6 copy.86
  228.2 1.8 fusion.84
  230.0 2.8 bitcast_convert_fusion.1
  232.8 2.0 copy.105
  234.9 3.2 copy.103
  243.3 6.8 %pad_maximum_fusion = bf16[16,2,48,768]{3,1,2,0:T(2,128)(2,1)} fusion(bf16[16,1,48,768]{3,1,2,0:T(2,128)(2,1)S(1)} %copy-done.20, bf16[16,1,48,768]{3,1,2,0:T(2,128)(2,1)S(1)} %copy-done.18), kind=kLoop, calls=%fused_computation.20 | loop fusion | flops 4718592 | bytes 4718592 | tf_op jit(solution)/shard_map/stack | solution.py:63
  250.1 3.1 subtract_convert_fusion.1
  253.1 15.5 %all-to-all-done.5 = bf16[16,2,48,768]{3,2,1,0:T(8,128)(2,1)} async-done(((bf16[16,2,48,768]{3,2,1,0:T(8,128)(2,1)}), bf16[16,2,48,768]{3,2,1,0:T(8,128)(2,1)}, u32[]{:S(2)}, u32[]{:S(2)}) %all-to-all-start.5) | async-done | bytes 2359328 | tf_op jit(solution)/shard_map/all_to_all | solution.py:61
  268.6 5.2 %all-to-all-start.2 = ((bf16[16,2,48,768]{3,1,2,0:T(2,128)(2,1)}), bf16[16,2,48,768]{3,1,2,0:T(2,128)(2,1)}, u32[]{:S(2)}, u32[]{:S(2)}) async-start(bf16[16,2,48,768]{3,1,2,0:T(2,128)(2,1)} %pad_maximum_fusion), calls=%async_computation.2 | async-start | bytes 4718592 | tf_op jit(solution)/shard_map/all_to_all | solution.py:65
  273.9 2.9 fusion.92
  280.9 3.6 copy.106
  286.7 3.6 copy.107
  292.1 2.6 bitcast_convert_fusion.3
  294.8 2.0 copy.98
  296.8 3.4 copy.96
  305.5 6.7 %pad_maximum_fusion.3 = bf16[16,2,48,768]{3,1,2,0:T(2,128)(2,1)} fusion(bf16[16,1,48,768]{3,1,2,0:T(2,128)(2,1)S(1)} %copy-done.21, bf16[16,1,48,768]{3,1,2,0:T(2,128)(2,1)S(1)} %copy-done.19), kind=kLoop, calls=%fused_computation.23 | loop fusion | flops 4718592 | bytes 4718592 | tf_op jit(solution)/shard_map/stack | solution.py:63
  312.2 14.6 %all-to-all-done.2 = bf16[16,2,48,768]{3,1,2,0:T(2,128)(2,1)} async-done(((bf16[16,2,48,768]{3,1,2,0:T(2,128)(2,1)}), bf16[16,2,48,768]{3,1,2,0:T(2,128)(2,1)}, u32[]{:S(2)}, u32[]{:S(2)}) %all-to-all-start.2) | async-done | bytes 2359328 | tf_op jit(solution)/shard_map/all_to_all | solution.py:65
  326.9 5.2 all-to-all-start.8
  332.1 2.9 fusion.89
  341.9 3.6 copy.99
  347.7 3.7 copy.100
  351.4 1.8 fusion.82
  353.2 2.6 bitcast_convert_fusion.5
  355.9 2.4 copy.91
  358.3 9.1 %pad_maximum_fusion.2 = bf16[16,2,48,768]{3,1,2,0:T(2,128)(2,1)} fusion(bf16[16,1,48,768]{3,1,2,0:T(2,128)(2,1)} %copy.100, bf16[16,1,48,768]{3,1,2,0:T(2,128)(2,1)} %copy.99), kind=kLoop, calls=%fused_computation.22 | loop fusion | flops 4718592 | bytes 4718592 | tf_op jit(solution)/shard_map/stack | solution.py:63
  367.4 17.7 %all-to-all-done.8 = bf16[16,2,48,768]{3,1,2,0:T(2,128)(2,1)} async-done(((bf16[16,2,48,768]{3,1,2,0:T(2,128)(2,1)}), bf16[16,2,48,768]{3,1,2,0:T(2,128)(2,1)}, u32[]{:S(2)}, u32[]{:S(2)}) %all-to-all-start.8) | async-done | bytes 2359328 | tf_op jit(solution)/shard_map/all_to_all | solution.py:65
  385.1 4.9 all-to-all-start.6
  391.4 3.0 copy.89
  394.4 2.2 fusion.25
  404.8 2.3 copy.92
  409.4 2.3 copy.93
  411.8 6.9 %pad_maximum_fusion.1 = bf16[16,2,48,768]{3,1,2,0:T(2,128)(2,1)} fusion(bf16[16,1,48,768]{3,1,2,0:T(2,128)(2,1)S(1)} %copy.93, bf16[16,1,48,768]{3,1,2,0:T(2,128)(2,1)S(1)} %copy.92), kind=kLoop, calls=%fused_computation.21 | loop fusion | flops 4718592 | bytes 4718592 | tf_op jit(solution)/shard_map/stack | solution.py:63
  418.7 24.4 %all-to-all-done.6 = bf16[16,2,48,768]{3,1,2,0:T(2,128)(2,1)} async-done(((bf16[16,2,48,768]{3,1,2,0:T(2,128)(2,1)}), bf16[16,2,48,768]{3,1,2,0:T(2,128)(2,1)}, u32[]{:S(2)}, u32[]{:S(2)}) %all-to-all-start.6) | async-done | bytes 2359328 | tf_op jit(solution)/shard_map/all_to_all | solution.py:65
  443.1 4.9 all-to-all-start.4
  448.0 5.6 %copy.108 = bf16[16,2,48,768]{3,0,1,2:T(8,128)(2,1)} copy(bf16[16,2,48,768]{3,1,2,0:T(2,128)(2,1)} %all-to-all-done.2) | data formatting | bytes 4718592 | tf_op jit(solution)/shard_map/all_to_all | solution.py:65
  453.7 5.6 %copy.111 = bf16[16,2,48,768]{3,0,1,2:T(8,128)(2,1)} copy(bf16[16,2,48,768]{3,1,2,0:T(2,128)(2,1)} %all-to-all-done.8) | data formatting | bytes 4718592 | tf_op jit(solution)/shard_map/all_to_all | solution.py:65
  459.3 5.6 %copy.110 = bf16[16,2,48,768]{3,0,1,2:T(8,128)(2,1)} copy(bf16[16,2,48,768]{3,1,2,0:T(2,128)(2,1)} %all-to-all-done.6) | data formatting | bytes 4718592 | tf_op jit(solution)/shard_map/all_to_all | solution.py:65
  464.9 36.2 %all-to-all-done.4 = bf16[16,2,48,768]{3,1,2,0:T(2,128)(2,1)S(1)} async-done(((bf16[16,2,48,768]{3,1,2,0:T(2,128)(2,1)}), bf16[16,2,48,768]{3,1,2,0:T(2,128)(2,1)S(1)}, u32[]{:S(2)}, u32[]{:S(2)}) %all-to-all-start.4) | async-done | bytes 2359328 | tf_op jit(solution)/shard_map/all_to_all | solution.py:65
  501.1 3.9 copy.109
  505.0 18.6 %bitcast_convert_fusion = bf16[48,768,512]{2,1,0:T(8,128)(2,1)} fusion(bf16[16,2,48,768]{3,0,1,2:T(8,128)(2,1)} %copy.111, bf16[16,2,48,768]{3,0,1,2:T(8,128)(2,1)} %copy.110, bf16[16,2,48,768]{3,0,1,2:T(8,128)(2,1)} %copy.109, bf16[16,2,48,768]{3,0,1,2:T(8,128)(2,1)} %copy.108, bf16[64,1,512]{2,0,1:T(8,128)(2,1)S(1)} %copy-done.30, ...), kind=kOutput, calls=%fused_computation | convolution fusion | flops 4888526848 | bytes 47316992 | tf_op jit(solution)/shard_map/dot_general | solution.py:67
  (118 shorter events, 53.6 us)
Async XLA Ops:
  0.0 13.6 %copy-start.35 = (s32[48,768]{1,0:T(8,128)S(1)}, s32[48,768]{1,0:T(8,128)}, u32[]{:S(2)}) copy-start(s32[48,768]{1,0:T(8,128)} %param.3) | copy-start | bytes 442372
  2.1 10.9 %all-to-all-start = ((bf16[16,2,1152]{2,1,0:T(2,128)(2,1)}), bf16[16,2,1152]{2,1,0:T(2,128)(2,1)S(1)}, u32[]{:S(2)}, u32[]{:S(2)}) async-start(bf16[16,2,1152]{2,1,0:T(2,128)(2,1)} %reshape.174), calls=%async_computation | async-start | bytes 147456 | tf_op jit(solution)/shard_map/all_to_all | solution.py:50
  9.2 147.8 %copy-start.29 = (bf16[64,1,512]{2,0,1:T(8,128)(2,1)}, bf16[64,1,512]{2,0,1:T(8,128)(2,1)S(1)}, u32[]{:S(2)}) copy-start(bf16[64,1,512]{2,0,1:T(8,128)(2,1)S(1)} %fusion.63) | copy-start | bytes 196612
  9.8 147.3 %copy-start.31 = (bf16[64,1,512]{2,0,1:T(8,128)(2,1)}, bf16[64,1,512]{2,0,1:T(8,128)(2,1)S(1)}, u32[]{:S(2)}) copy-start(bf16[64,1,512]{2,0,1:T(8,128)(2,1)S(1)} %multiply_convert_fusion.5) | copy-start | bytes 196612
  33.5 60.2 %all-to-all-start.3 = ((bf16[16,2,48,768]{3,2,1,0:T(8,128)(2,1)}), bf16[16,2,48,768]{3,2,1,0:T(8,128)(2,1)}, u32[]{:S(2)}, u32[]{:S(2)}) async-start(bf16[16,2,48,768]{3,2,1,0:T(8,128)(2,1)} %copy.87), calls=%async_computation.3 | async-start | bytes 4718592 | tf_op jit(solution)/shard_map/all_to_all | solution.py:61
  93.7 58.0 %all-to-all-start.1 = ((bf16[16,2,48,768]{3,2,1,0:T(8,128)(2,1)}), bf16[16,2,48,768]{3,2,1,0:T(8,128)(2,1)}, u32[]{:S(2)}, u32[]{:S(2)}) async-start(bf16[16,2,48,768]{3,2,1,0:T(8,128)(2,1)} %copy.80), calls=%async_computation.1 | async-start | bytes 4718592 | tf_op jit(solution)/shard_map/all_to_all | solution.py:61
  151.7 58.4 %all-to-all-start.7 = ((bf16[16,2,48,768]{3,2,1,0:T(8,128)(2,1)}), bf16[16,2,48,768]{3,2,1,0:T(8,128)(2,1)}, u32[]{:S(2)}, u32[]{:S(2)}) async-start(bf16[16,2,48,768]{3,2,1,0:T(8,128)(2,1)} %copy.101), calls=%async_computation.7 | async-start | bytes 4718592 | tf_op jit(solution)/shard_map/all_to_all | solution.py:61
  178.8 1.9 copy-start.12
  188.4 1.7 copy-start.2
  188.4 2.0 copy-start.13
  196.6 19.0 %copy-start.24 = (f32[768,768]{1,0:T(8,128)S(1)}, f32[768,768]{1,0:T(8,128)}, u32[]{:S(2)}) copy-start(f32[768,768]{1,0:T(8,128)} %get-tuple-element.28) | copy-start | bytes 7077892
  196.6 19.0 %copy-start.34 = (bf16[768,768]{1,0:T(8,128)(2,1)S(1)}, bf16[768,768]{1,0:T(8,128)(2,1)}, u32[]{:S(2)}) copy-start(bf16[768,768]{1,0:T(8,128)(2,1)} %get-tuple-element.27) | copy-start | bytes 3538948
  210.1 58.6 %all-to-all-start.5 = ((bf16[16,2,48,768]{3,2,1,0:T(8,128)(2,1)}), bf16[16,2,48,768]{3,2,1,0:T(8,128)(2,1)}, u32[]{:S(2)}, u32[]{:S(2)}) async-start(bf16[16,2,48,768]{3,2,1,0:T(8,128)(2,1)} %copy.94), calls=%async_computation.5 | async-start | bytes 4718592 | tf_op jit(solution)/shard_map/all_to_all | solution.py:61
  215.6 1.7 copy-start.22
  215.6 2.0 copy-start.25
  230.0 2.8 copy-start.10
  238.1 1.7 copy-start.3
  238.1 2.0 copy-start.11
  240.0 10.0 %copy-start.14 = (bf16[768,768]{1,0:T(8,128)(2,1)}, bf16[768,768]{1,0:T(8,128)(2,1)S(1)}, u32[]{:S(2)}) copy-start(bf16[768,768]{1,0:T(8,128)(2,1)S(1)} %fusion.30) | copy-start | bytes 3538948
  240.4 1.1 copy-start.26
  240.5 2.1 copy-start.18
  240.5 2.8 copy-start.20
  268.6 58.2 %all-to-all-start.2 = ((bf16[16,2,48,768]{3,1,2,0:T(2,128)(2,1)}), bf16[16,2,48,768]{3,1,2,0:T(2,128)(2,1)}, u32[]{:S(2)}, u32[]{:S(2)}) async-start(bf16[16,2,48,768]{3,1,2,0:T(2,128)(2,1)} %pad_maximum_fusion), calls=%async_computation.2 | async-start | bytes 4718592 | tf_op jit(solution)/shard_map/all_to_all | solution.py:65
  273.9 2.9 copy-start.23
  273.9 2.9 copy-start.33
  276.8 1.3 copy-start.15
  276.8 1.6 copy-start.27
  292.1 2.7 copy-start.5
  300.3 2.1 copy-start
  300.3 2.4 copy-start.6
  302.7 2.1 copy-start.19
  302.7 2.8 copy-start.21
  326.9 58.2 %all-to-all-start.8 = ((bf16[16,2,48,768]{3,1,2,0:T(2,128)(2,1)}), bf16[16,2,48,768]{3,1,2,0:T(2,128)(2,1)}, u32[]{:S(2)}, u32[]{:S(2)}) async-start(bf16[16,2,48,768]{3,1,2,0:T(2,128)(2,1)} %pad_maximum_fusion.3), calls=%async_computation.8 | async-start | bytes 4718592 | tf_op jit(solution)/shard_map/all_to_all | solution.py:65
  332.1 2.9 copy-start.16
  332.1 2.9 copy-start.28
  335.0 1.7 copy-start.1
  335.0 2.0 copy-start.7
  353.2 2.7 copy-start.8
  385.1 58.0 %all-to-all-start.6 = ((bf16[16,2,48,768]{3,1,2,0:T(2,128)(2,1)}), bf16[16,2,48,768]{3,1,2,0:T(2,128)(2,1)}, u32[]{:S(2)}, u32[]{:S(2)}) async-start(bf16[16,2,48,768]{3,1,2,0:T(2,128)(2,1)} %pad_maximum_fusion.2), calls=%async_computation.6 | async-start | bytes 4718592 | tf_op jit(solution)/shard_map/all_to_all | solution.py:65
  396.7 1.3 copy-start.17
  397.9 1.7 copy-start.4
  397.9 2.0 copy-start.9
  443.1 57.9 %all-to-all-start.4 = ((bf16[16,2,48,768]{3,1,2,0:T(2,128)(2,1)}), bf16[16,2,48,768]{3,1,2,0:T(2,128)(2,1)S(1)}, u32[]{:S(2)}, u32[]{:S(2)}) async-start(bf16[16,2,48,768]{3,1,2,0:T(2,128)(2,1)} %pad_maximum_fusion.1), calls=%async_computation.4 | async-start | bytes 4718592 | tf_op jit(solution)/shard_map/all_to_all | solution.py:65
  464.9 40.1 %copy-start.30 = (bf16[64,1,512]{2,0,1:T(8,128)(2,1)S(1)}, bf16[64,1,512]{2,0,1:T(8,128)(2,1)}, u32[]{:S(2)}) copy-start(bf16[64,1,512]{2,0,1:T(8,128)(2,1)} %copy-done.29) | copy-start | bytes 196612
  464.9 40.1 %copy-start.32 = (bf16[64,1,512]{2,0,1:T(8,128)(2,1)S(1)}, bf16[64,1,512]{2,0,1:T(8,128)(2,1)}, u32[]{:S(2)}) copy-start(bf16[64,1,512]{2,0,1:T(8,128)(2,1)} %copy-done.31) | copy-start | bytes 196612

commit v2 on v1

v2 whole, which is shorter than its diff:
```python
import functools
import math

import jax
import jax.numpy as jnp
from jax import lax
from jax.experimental import pallas as pl
from jax.experimental.pallas import tpu as pltpu
from jax.sharding import PartitionSpec as P

NT = 512
NF = 64
F_LO = 8
TILE = 16


def tables():
    bins = F_LO + jnp.arange(NF, dtype=jnp.int32)
    times = jnp.arange(NT, dtype=jnp.int32)
    phase = bins[:, None] * times[None, :] % NT
    angle = phase.astype(jnp.float32) * jnp.float32(2.0 * math.pi / NT)
    cosine = (jnp.cos(angle) / math.sqrt(NT)).astype(jnp.bfloat16)
    sine = (jnp.sin(angle) / math.sqrt(NT)).astype(jnp.bfloat16)
    return jnp.stack([cosine, -sine], axis=1)


def mm(a, b):
    return jnp.dot(a, b, preferred_element_type=jnp.float32)


def kept(i, j, s, r, group):
    diff = i ^ j
    part = (r > s).astype(jnp.int32)
    bit = 1
    while bit < group:
        part = jnp.where(diff >= bit, (i // bit) % 2, part)
        bit *= 2
    return part == 1


def pair_mask(rows, group, first_row, count):
    s = lax.broadcasted_iota(jnp.int32, (count, rows * group), 0) + first_row
    r = lax.broadcasted_iota(jnp.int32, (count, rows * group), 1)
    return kept(s // rows, r // rows, s, r, group), s == r


def chain_kernel(rows, slot, packed_in, packed_out, *refs):
    count = 4 if packed_in else 1
    ins, ratio, out, (br, bi, fr, fi) = refs[:count], refs[count], refs[count + 1], refs[count + 2 :]
    order = br.shape[0]
    half = order // 2
    n = order // rows
    inv = 1.0 / math.sqrt(order)
    f32, b16 = jnp.float32, jnp.bfloat16
    if packed_in or packed_out:
        mask, diag = pair_mask(rows, n // 2, 0, half)
    if packed_in:
        re, im, mix, extra = ins
        for ref, b in ((re, br), (im, bi)):
            upper = ref[: n // 2].reshape(half, half).astype(f32)
            lower = ref[n // 2 :].reshape(half, half).astype(f32)
            cross = (upper + lower.T) * ratio[:half, half:]
            b[:half, half:] = cross.astype(b16)
            b[half:, :half] = cross.T.astype(b16)
        for h in range(2):
            pick = slice(h * half, (h + 1) * half)
            both = mix[h * (n // 2) : (h + 1) * (n // 2)].reshape(half, half).astype(f32)
            tr = jnp.where(mask, 0.0, both)
            br[pick, pick] = ((tr + tr.T) * ratio[pick, pick]).astype(b16)
            line = jnp.sum(
                extra[h * (n // 2) : (h + 1) * (n // 2), slot : slot + 1].astype(f32), axis=0
            )
            ti = jnp.where(mask, both, 0.0)
            ti = ti + ti.T + jnp.where(diag, 2.0 * line, 0.0)
            bi[pick, pick] = (ti * ratio[pick, pick]).astype(b16)
    else:
        for c, b in ((0, br), (1, bi)):
            y = ins[0][:, c].reshape(order, order).astype(f32)
            b[...] = ((y + y.T) * ratio[...]).astype(b16)
    step = 256 if order % 256 == 0 else order
    for t in range(0, order, step):
        ar, ai = br[t : t + step], bi[t : t + step]
        fr[t : t + step] = (mm(ar, br[...]) - mm(ai, bi[...])) * inv
        fi[t : t + step] = (mm(ar, bi[...]) + mm(ai, br[...])) * inv
    gr = (fr[...] - br[...].astype(f32)).astype(b16)
    gi = (fi[...] - bi[...].astype(f32)).astype(b16)
    br[...] = gr
    bi[...] = gi
    for t in range(0, order, step):
        cr, ci = fr[t : t + step], fi[t : t + step]
        ar, ai = cr.astype(b16), ci.astype(b16)
        pr = cr + (mm(ar, br[...]) - mm(ai, bi[...])) * inv
        pi = ci + (mm(ar, bi[...]) + mm(ai, br[...])) * inv
        fr[t : t + step] = pr
        fi[t : t + step] = pi
    if packed_out:
        out[:, 3 * rows :] = jnp.zeros((n, TILE, half), b16)
        for h in range(2):
            own = slice(h * half, (h + 1) * half)
            other = slice((1 - h) * half, (2 - h) * half)
            dst = slice(h * (n // 2), (h + 1) * (n // 2))
            shape = (n // 2, rows, half)
            out[dst, :rows] = fr[own, other].astype(b16).reshape(shape)
            out[dst, rows : 2 * rows] = fi[own, other].astype(b16).reshape(shape)
            pr, pi = fr[own, own], fi[own, own]
            out[dst, 2 * rows : 3 * rows] = jnp.where(mask, pi, pr).astype(b16).reshape(shape)
            line = jnp.sum(jnp.where(diag, pi, 0.0), axis=0, keepdims=True)
            tile = jnp.where(
                lax.broadcasted_iota(jnp.int32, (TILE, half), 0) == slot,
                jnp.broadcast_to(line, (TILE, half)),
                0.0,
            ).astype(b16)
            out[dst, 3 * rows :] = jnp.broadcast_to(tile[None], (n // 2, TILE, half))
    else:
        out[:, 0] = fr[...].astype(b16).reshape(n, rows, order)
        out[:, 1] = fi[...].astype(b16).reshape(n, rows, order)


def chain(got, ratio, rows, order, slot_in, total_in, slot_out, packed_out):
    n, half = order // rows, order // 2
    packed_in = total_in > 0
    slot = slot_in if packed_in else slot_out
    if packed_in:
        specs = [
            pl.BlockSpec((n, rows, half), functools.partial(lambda b, i: (0, b, 0), 3 * slot_in + c))
            for c in range(3)
        ]
        last = 3 * rows * total_in // TILE
        specs.append(pl.BlockSpec((n, TILE, half), lambda i: (0, last, 0)))
        args = [got] * 4 + [ratio]
    else:
        specs = [pl.BlockSpec((n, 2, rows, order), lambda i: (0, 0, 0, 0))]
        args = [got, ratio]
    specs.append(pl.BlockSpec((order, order), lambda i: (0, 0)))
    shape = (n, 3 * rows + TILE, half) if packed_out else (n, 2, rows, order)
    return pl.pallas_call(
        functools.partial(chain_kernel, rows, slot, packed_in, packed_out),
        out_shape=jax.ShapeDtypeStruct(shape, jnp.bfloat16),
        grid=(1,),
        in_specs=specs,
        out_specs=pl.BlockSpec(shape, lambda i: (0,) * len(shape)),
        scratch_shapes=[
            pltpu.VMEM((order, order), jnp.bfloat16),
            pltpu.VMEM((order, order), jnp.bfloat16),
            pltpu.VMEM((order, order), jnp.float32),
            pltpu.VMEM((order, order), jnp.float32),
        ],
        compiler_params=pltpu.CompilerParams(vmem_limit_bytes=48 * 1024 * 1024),
        cost_estimate=pl.CostEstimate(
            flops=16 * order**3, bytes_accessed=8 * order * order, transcendentals=0
        ),
    )(*args)


def side(ref, upper, inside):
    half = ref.shape[-1] // 2
    low, high = ref[..., :half].astype(jnp.float32), ref[..., half:].astype(jnp.float32)
    return jnp.where(upper == inside, low, high)


def give_kernel(rows, group, whole, where_ref, x, *outs):
    me, upper = where_ref[0], where_ref[1] == 1
    turned = outs[-1]
    n, half = 2 * group, rows * group
    if whole:
        mask, diag = pair_mask(rows, group, me * rows, rows)
        re, im = side(x.at[:, 0, 0], upper, True), side(x.at[:, 0, 1], upper, True)
        block = jnp.where(diag[None], 0.0, jnp.where(mask[None], re, im))
    else:
        block = x[...].astype(jnp.float32)
    turned[...] = block.reshape(n * rows, half).T.astype(jnp.bfloat16).reshape(group, rows, n * rows)
    for m in range(group):
        outs[m][...] = turned[me ^ m]


def give(x, where, rows, group, count, whole):
    n, half = 2 * group, rows * group
    if whole:
        spec = pl.BlockSpec((n, 1, 2, rows, 2 * half), lambda f, w: (0, f + 1, 0, 0, 0))
    else:
        spec = pl.BlockSpec((n, rows, half), lambda f, w: (0, 3 * f + 2, 0))
    return pl.pallas_call(
        functools.partial(give_kernel, rows, group, whole),
        out_shape=[jax.ShapeDtypeStruct((rows, count * n * rows), jnp.bfloat16)] * group,
        grid_spec=pltpu.PrefetchScalarGridSpec(
            num_scalar_prefetch=1,
            grid=(count,),
            in_specs=[spec],
            out_specs=[pl.BlockSpec((rows, n * rows), lambda f, w: (0, f))] * group,
            scratch_shapes=[pltpu.VMEM((group, rows, n * rows), jnp.bfloat16)],
        ),
        compiler_params=pltpu.CompilerParams(vmem_limit_bytes=48 * 1024 * 1024),
        cost_estimate=pl.CostEstimate(
            flops=0, bytes_accessed=count * 16 * rows * n * half, transcendentals=0
        ),
    )(where, x)


def place(pieces, me, rows, group, spread, other):
    for m in range(group):
        spread[me ^ m] = pieces[m][...].astype(jnp.float32)
    for j in range(group):
        for d in range(2 * group):
            other[d, :, j * rows : (j + 1) * rows] = spread[j, :, d * rows : (d + 1) * rows]


def pack_kernel(rows, group, count, where_ref, x, *refs):
    me, upper = where_ref[0], where_ref[1] == 1
    pieces, out, (spread, other) = refs[:group], refs[group], refs[group + 1 :]
    n, half = 2 * group, rows * group
    b16 = jnp.bfloat16
    f = pl.program_id(0)
    place(pieces, me, rows, group, spread, other)
    mask, diag = pair_mask(rows, group, me * rows, rows)
    base = pl.multiple_of(f * 3 * rows, 16)
    for c in range(2):
        out[:, pl.ds(base + c * rows, rows)] = side(x.at[:, 0, c], upper, False).astype(b16)
    re, im = side(x.at[:, 0, 0], upper, True), side(x.at[:, 0, 1], upper, True)
    keep = jnp.where(mask[None], im, re) + other[...]
    out[:, pl.ds(base + 2 * rows, rows)] = keep.astype(b16)
    line = jnp.sum(jnp.where(diag[None], im, 0.0), axis=1, keepdims=True)
    slot = lax.broadcasted_iota(jnp.int32, (n, TILE, half), 1) == f
    tile = jnp.where(slot, jnp.broadcast_to(line, (n, TILE, half)), 0.0)

    @pl.when(f == 0)
    def _():
        out[:, count * 3 * rows :] = jnp.zeros((n, TILE, half), b16)

    old = out[:, count * 3 * rows :].astype(jnp.float32)
    out[:, count * 3 * rows :] = (old + tile).astype(b16)


def pack(x, pieces, where, rows, group, count):
    n, half = 2 * group, rows * group
    shape = (n, count * 3 * rows + TILE, half)
    return pl.pallas_call(
        functools.partial(pack_kernel, rows, group, count),
        out_shape=jax.ShapeDtypeStruct(shape, jnp.bfloat16),
        grid_spec=pltpu.PrefetchScalarGridSpec(
            num_scalar_prefetch=1,
            grid=(count,),
            in_specs=[pl.BlockSpec((n, 1, 2, rows, 2 * half), lambda f, w: (0, f + 1, 0, 0, 0))]
            + [pl.BlockSpec((rows, n * rows), lambda f, w: (0, f))] * group,
            out_specs=pl.BlockSpec(shape, lambda f, w: (0, 0, 0)),
            scratch_shapes=[
                pltpu.VMEM((group, rows, n * rows), jnp.float32),
                pltpu.VMEM((n, rows, half), jnp.float32),
            ],
        ),
        compiler_params=pltpu.CompilerParams(vmem_limit_bytes=48 * 1024 * 1024),
        cost_estimate=pl.CostEstimate(
            flops=0, bytes_accessed=count * 20 * rows * n * half, transcendentals=0
        ),
    )(where, x, *pieces)


def unpack_kernel(rows, group, where_ref, re_ref, im_ref, mix_ref, tile_ref, *refs):
    me, upper = where_ref[0], where_ref[1] == 1
    pieces, out, (spread, other) = refs[:group], refs[group], refs[group + 1 :]
    n, half = 2 * group, rows * group
    b16, f32 = jnp.bfloat16, jnp.float32
    f = pl.program_id(0)
    place(pieces, me, rows, group, spread, other)
    mask, diag = pair_mask(rows, group, me * rows, rows)
    slot = lax.broadcasted_iota(jnp.int32, (n, TILE, half), 1) == f
    line = jnp.sum(jnp.where(slot, tile_ref[...].astype(f32), 0.0), axis=1, keepdims=True)
    mix, rest = mix_ref[...].astype(f32), other[...]
    for c, ref in ((0, re_ref), (1, im_ref)):
        if c == 0:
            inner = jnp.where(mask[None], rest, mix)
        else:
            inner = jnp.where(diag[None], line, jnp.where(mask[None], mix, rest))
        outer = ref[...].astype(f32)
        out[:, c, :, :half] = jnp.where(upper, inner, outer).astype(b16)
        out[:, c, :, half:] = jnp.where(upper, outer, inner).astype(b16)


def unpack(back, pieces, where, rows, group, count):
    n, half = 2 * group, rows * group
    last = 3 * rows * count // TILE
    return pl.pallas_call(
        functools.partial(unpack_kernel, rows, group),
        out_shape=jax.ShapeDtypeStruct((count * n, 2, rows, 2 * half), jnp.bfloat16),
        grid_spec=pltpu.PrefetchScalarGridSpec(
            num_scalar_prefetch=1,
            grid=(count,),
            in_specs=[
                pl.BlockSpec((n, rows, half), functools.partial(lambda c, f, w: (0, 3 * f + c, 0), c))
                for c in range(3)
            ]
            + [pl.BlockSpec((n, TILE, half), lambda f, w: (0, last, 0))]
            + [pl.BlockSpec((rows, n * rows), lambda f, w: (0, f))] * group,
            out_specs=pl.BlockSpec((n, 2, rows, 2 * half), lambda f, w: (f, 0, 0, 0)),
            scratch_shapes=[
                pltpu.VMEM((group, rows, n * rows), jnp.float32),
                pltpu.VMEM((n, rows, half), jnp.float32),
            ],
        ),
        compiler_params=pltpu.CompilerParams(vmem_limit_bytes=48 * 1024 * 1024),
        cost_estimate=pl.CostEstimate(
            flops=0, bytes_accessed=count * 20 * rows * n * half, transcendentals=0
        ),
    )(where, *[back] * 4, *pieces)


def swap(pieces, n):
    return list(pieces[:1]) + [
        lax.ppermute(piece, "tile", [(i, i ^ m) for i in range(n)])
        for m, piece in enumerate(pieces)
        if m
    ]


def a2a(x):
    return lax.all_to_all(x, "tile", split_axis=0, concat_axis=0, tiled=True)


def spectrum_of(part, traces):
    return lax.dot_general(
        part, traces, (((part.ndim - 1,), (2,)), ((), ())), preferred_element_type=jnp.float32
    )


def generic(traces, weight, forward, n):
    rows, order = weight.shape
    mirror = lax.all_to_all(
        weight.astype(jnp.bfloat16), "tile", split_axis=1, concat_axis=0, tiled=True
    )
    share = weight / (weight + mirror.T.astype(jnp.float32))
    returned = []
    for chunk in range(NF // n):
        part = forward[chunk * n : (chunk + 1) * n]
        got = a2a((share * spectrum_of(part, traces)).astype(jnp.bfloat16))
        y = [got[:, c].reshape(order, order).astype(jnp.float32) for c in range(2)]
        br, bi = ((v + v.T).astype(jnp.bfloat16) for v in y)
        inv = 1.0 / math.sqrt(order)
        fr, fi = (mm(br, br) - mm(bi, bi)) * inv, (mm(br, bi) + mm(bi, br)) * inv
        gr, gi = (fr - br).astype(jnp.bfloat16), (fi - bi).astype(jnp.bfloat16)
        ar, ai = fr.astype(jnp.bfloat16), fi.astype(jnp.bfloat16)
        parts = [
            fr + (mm(ar, gr) - mm(ai, gi)) * inv,
            fi + (mm(ar, gi) + mm(ai, gr)) * inv,
        ]
        back = jnp.stack([v.astype(jnp.bfloat16).reshape(n, rows, order) for v in parts], 1)
        returned.append(a2a(back))
    return jnp.concatenate(returned, 0)


def pipelined(traces, weight, forward, n):
    order = traces.shape[1]
    rows = traces.shape[0]
    half, group = order // 2, n // 2
    per = NF // n
    b16 = jnp.bfloat16
    index = lax.axis_index("tile")
    where = jnp.stack([index % group, (index < group).astype(jnp.int32)])

    every = lax.all_gather(weight.astype(b16), "tile", axis=0, tiled=True).astype(jnp.float32)
    ratio = 1.0 / (every + every.T)
    part = forward.reshape(per, n, 2, NT).transpose(1, 0, 2, 3)
    mixed = (weight * spectrum_of(part, traces)).astype(b16)
    mixed, ratio = lax.optimization_barrier((mixed, ratio))

    whole = a2a(mixed[:, 0])
    rest = per - 1
    pieces = swap(give(mixed, where, rows, group, rest, True), n)
    got = a2a(pack(mixed, pieces, where, rows, group, rest))

    answers = [chain(whole, ratio, rows, order, 0, 0, 0, True)]
    for f in range(rest):
        answers.append(chain(got, ratio, rows, order, f, rest, f, f < rest - 1))

    def bring(fs):
        count = len(fs)
        if count > 1:
            tile = sum(answers[f][:, 3 * rows :] for f in fs)
            sent = jnp.concatenate([answers[f][:, : 3 * rows] for f in fs] + [tile], 1)
        else:
            sent = answers[fs[0]]
        back = a2a(sent)
        return back, swap(give(back, where, rows, group, count, False), n)

    early = bring([0])
    later = bring(list(range(1, per - 1)))
    early, final = lax.optimization_barrier((early, answers[-1]))
    returned = [
        unpack(*early, where, rows, group, 1),
        unpack(*later, where, rows, group, per - 2),
        a2a(final),
    ]
    return jnp.concatenate(returned, 0)


def body(traces, quality):
    rows, order = quality.shape
    n = order // rows
    forward = tables()
    weight = (quality + 1).astype(jnp.float32)
    if rows % 16 == 0 and order % 256 == 0 and n & (n - 1) == 0 and NF // n >= 3:
        returned = pipelined(traces, weight, forward, n)
    else:
        returned = generic(traces, weight, forward, n)
    result = lax.dot_general(
        returned, forward, (((0, 1), (0, 1)), ((), ())), preferred_element_type=jnp.float32
    )
    return result.astype(jnp.bfloat16)


def solution(mesh):
    in_specs = (P(("swath", "tile"), None, None), P(("swath", "tile"), None))
    out_specs = P(("swath", "tile"), None, None)
    return jax.shard_map(body, mesh=mesh, in_specs=in_specs, out_specs=out_specs, check_vma=False)
```

time: 533 us -> 511 us (0.959)
  the two profiles are of different devices: /device:TPU:15 before, /device:TPU:17 now
where the time goes in v2:
time: 511 us; the launch traced here: 503 us
  waiting for transfers between devices  270 us (53%)
  Pallas kernels  70.2 us (14%)
  starting transfers between devices  62 us (12%)
  matrix products  44 us (9%)
  other arithmetic  29.2 us (6%)
  between operations  14 us (3%)
  local copies, waits for them, and re-layouts  13.2 us (3%)
    all_to_all x5, waiting for transfers between devices, a2a(): return lax.all_to_all(x, 'tile', split_axis=0, concat_axis=0, tiled=True)  139 us
    ppermute x21, waiting for transfers between devices, swap(): lax.ppermute(piece, 'tile', [(i, i ^ m) for i in range(n)])  129 us
    pallas_call x4, Pallas kernels, chain(): pl.pallas_call(functools.partial(chain_kernel, rows, slot, packed_in, pac...  42.6 us
    ppermute x21, starting transfers between devices, swap(): lax.ppermute(piece, 'tile', [(i, i ^ m) for i in range(n)])  33 us
    all_to_all x5, starting transfers between devices, a2a(): return lax.all_to_all(x, 'tile', split_axis=0, concat_axis=0, tiled=True)  29 us
    dot_general x1, matrix products, spectrum_of(): lax.dot_general(part, traces, (((part.ndim - 1,), (2,)), ((), ())), prefe...  22.4 us
    dot_general x1, matrix products, body(): lax.dot_general(returned, forward, (((0, 1), (0, 1)), ((), ())), preferre...  21.6 us
    convert_element_type x1, other arithmetic, pipelined(): mixed = (weight * spectrum_of(part, traces)).astype(b16)  14.3 us
  transfers between devices with their start and end apart: 27, of which 20 were waited for; matrix products, arithmetic and copies ran while one was open for 8% of the time, Pallas kernels for 14%

profile of v2, /device:TPU:17, one launch (start us, length us, event | category | flops | bytes accessed | tf_op | source)
XLA Modules:
  0.0 502.6 jit_solution(10185075926103365774)
XLA Ops:
  6.5 1.5 fusion.25
  9.3 22.4 %fusion = f32[16,4,2,48,768]{4,0,3,2,1:T(8,128)} fusion(bf16[48,768,512]{2,1,0:T(8,128)(2,1)} %param.2, bf16[4,16,1,512]{3,1,2,0:T(8,128)(2,1)S(1)} %fusion.21, bf16[4,16,1,512]{3,1,2,0:T(8,128)(2,1)S(1)} %multiply_convert_fusion.3), kind=kOutput, calls=%fused_computation.1 | convolution fusion | flops 4832100352 | bytes 56754176 | tf_op jit(solution)/shard_map/dot_general | solution.py:319
  31.7 14.3 %fusion.2.x = bf16[16,4,2,48,768]{4,3,2,1,0:T(8,128)(2,1)} fusion(f32[16,4,2,48,768]{4,0,3,2,1:T(8,128)} %fusion, f32[48,768]{1,0:T(8,128)S(1)} %get-tuple-element.78), kind=kLoop, calls=%fused_computation.4 | loop fusion | flops 9437184 | bytes 28459008 | tf_op jit(solution)/shard_map/convert_element_type | solution.py:361
  46.0 1.8 all-gather.2.cloned.1.call-done
  47.8 1.6 copy.9
  49.4 0.6 copy.10
  50.1 1.7 fusion.4.refs_1_.refs_4_
  51.8 3.2 slice_bitcast_fusion
  55.0 5.7 %all-to-all-start = ((bf16[16,2,48,768]{3,2,1,0:T(8,128)(2,1)}), bf16[16,2,48,768]{3,2,1,0:T(8,128)(2,1)S(1)}, u32[]{:S(2)}, u32[]{:S(2)}) async-start(bf16[16,2,48,768]{3,2,1,0:T(8,128)(2,1)} %slice_bitcast_fusion), calls=%async_computation | async-start | bytes 4718592 | tf_op jit(solution)/shard_map/all_to_all | solution.py:315
  60.7 5.3 %shard_map.30 = (bf16[48,2304]{1,0:T(8,128)(2,1)S(1)}, bf16[48,2304]{1,0:T(8,128)(2,1)S(1)}, bf16[48,2304]{1,0:T(8,128)(2,1)S(1)}, bf16[48,2304]{1,0:T(8,128)(2,...) custom-call(s32[2]{0:T(128)S(1)} %pad_add_fusion.where_ref, ...), custom_call_target="tpu_custom_call" | custom-call | bytes 14155776 | tf_op jit(solution)/shard_map/pallas_call | solution.py:182
  66.4 1.2 collective-permute-start.8
  67.6 0.6 collective-permute-start.9
  68.2 1.2 collective-permute-start.10
  69.9 2.1 collective-permute-start.12
  72.0 8.2 %collective-permute-done.8.refs_2_ = bf16[48,2304]{1,0:T(8,128)(2,1)S(1)} collective-permute-done((bf16[48,2304]{1,0:T(8,128)(2,1)S(1)}, bf16[48,2304]{1,0:T(8,128)(2,1)S(1)}, u32[]{:S(2)}, u32[]{:S(2)}) %collective-permute-start.8) | collective-permute-done | bytes 221216 | tf_op jit(solution)/shard_map/ppermute | solution.py:308
  80.2 5.4 %collective-permute-start.13 = (bf16[48,2304]{1,0:T(8,128)(2,1)S(1)}, bf16[48,2304]{1,0:T(8,128)(2,1)S(1)}, u32[]{:S(2)}, u32[]{:S(2)}) collective-permute-start(bf16[48,2304]{1,0:T(8,128)(2,1)S(1)} %get-tuple-element.58), channel_id=1, source_target_pairs={{0,7},{1,6},{2,5},{3,4},{4,3},{5,2},{6,1},{7,0},{8,15},{9,14},{10,... | collective-permute-start | bytes 663560 | tf_op jit(solution)/shard_map/ppermute | solution.py:308
  85.5 0.6 collective-permute-done.9.refs_3_
  86.2 19.5 %collective-permute-done.10.refs_4_ = bf16[48,2304]{1,0:T(8,128)(2,1)S(1)} collective-permute-done((bf16[48,2304]{1,0:T(8,128)(2,1)S(1)}, bf16[48,2304]{1,0:T(8,128)(2,1)S(1)}, u32[]{:S(2)}, u32[]{:S(2)}) %collective-permute-start.10) | collective-permute-done | bytes 221216 | tf_op jit(solution)/shard_map/ppermute | solution.py:308
  105.7 5.7 %collective-permute-done.11.refs_5_ = bf16[48,2304]{1,0:T(8,128)(2,1)S(1)} collective-permute-done((bf16[48,2304]{1,0:T(8,128)(2,1)S(1)}, bf16[48,2304]{1,0:T(8,128)(2,1)S(1)}, u32[]{:S(2)}, u32[]{:S(2)}) %collective-permute-start.11) | collective-permute-done | bytes 221216 | tf_op jit(solution)/shard_map/ppermute | solution.py:308
  111.4 6.7 %collective-permute-done.12.refs_6_ = bf16[48,2304]{1,0:T(8,128)(2,1)S(1)} collective-permute-done((bf16[48,2304]{1,0:T(8,128)(2,1)S(1)}, bf16[48,2304]{1,0:T(8,128)(2,1)S(1)}, u32[]{:S(2)}, u32[]{:S(2)}) %collective-permute-start.12) | collective-permute-done | bytes 221216 | tf_op jit(solution)/shard_map/ppermute | solution.py:308
  118.1 5.0 collective-permute-done.13.refs_7_
  123.1 10.3 %shard_map.31 = bf16[16,448,384]{2,1,0:T(8,128)(2,1)} custom-call(s32[2]{0:T(128)S(1)} %pad_add_fusion.where_ref, bf16[16,4,2,48,768]{4,3,2,1,0:T(8,128)(2,1)} %fusion.2.x, bf16[48,2304]{1,0:T(8,128)(2,1)S(1)} %get-tuple-element.51.refs_0_, bf16[48,2304]{1,0:T(8,128)(2,1)S(1)} %collective-permute-done.7.refs_1_, ...), custom_call_target="tpu_custom_call" | custom-call | bytes 17694720 | tf_op jit(solution)/shard_map/pallas_call | solution.py:236
  133.4 4.7 all-to-all-start.2
  138.2 10.1 %shard_map.28 = bf16[16,160,384]{2,1,0:T(8,128)(2,1)S(1)} custom-call(bf16[16,2,48,768]{3,2,1,0:T(8,128)(2,1)S(1)} %all-to-all-done.refs_0_, f32[768,768]{1,0:T(8,128)} %fusion.4.refs_1_.refs_4_), custom_call_target="tpu_custom_call" | custom-call | flops 7247757312 | bytes 4718592 | tf_op jit(solution)/shard_map/pallas_call | solution.py:136
  148.3 1.3 copy-done.5
  149.6 108.4 %all-to-all-done.2.refs_0_.refs_1_.refs_2_.refs_3_ = bf16[16,448,384]{2,1,0:T(8,128)(2,1)} async-done(((bf16[16,448,384]{2,1,0:T(8,128)(2,1)}), bf16[16,448,384]{2,1,0:T(8,128)(2,1)}, u32[]{:S(2)}, u32[]{:S(2)}) %all-to-all-start.2) | async-done | bytes 5505056 | tf_op jit(solution)/shard_map/all_to_all | solution.py:315
  258.0 5.6 %all-to-all-start.1 = ((bf16[16,160,384]{2,1,0:T(8,128)(2,1)}), bf16[16,160,384]{2,1,0:T(8,128)(2,1)S(1)}, u32[]{:S(2)}, u32[]{:S(2)}) async-start(bf16[16,160,384]{2,1,0:T(8,128)(2,1)} %copy-done.5), calls=%async_computation.1 | async-start | bytes 3932160 | tf_op jit(solution)/shard_map/all_to_all | solution.py:315
  263.6 1.7 copy-done.3
  265.3 10.9 %shard_map.35 = bf16[16,160,384]{2,1,0:T(8,128)(2,1)S(1)} custom-call(bf16[16,448,384]{2,1,0:T(8,128)(2,1)} %all-to-all-done.2.refs_0_.refs_1_.refs_2_.refs_3_, bf16[16,448,384]{2,1,0:T(8,128)(2,1)} %all-to-all-done.2.refs_0_.refs_1_.refs_2_.refs_3_, bf16[16,448,384]{2,1,0:T(8,128)(2,1)} %all-to-all-done.2.refs_0_.refs_1_.refs_2_.refs_3_, ...), custom_call_target="tpu_custom_call" | custom-call | flops 7247757312 | bytes 4718592 | tf_op jit(solution)/shard_map/pallas_call | solution.py:136
  276.3 11.1 %shard_map.34 = bf16[16,160,384]{2,1,0:T(8,128)(2,1)S(1)} custom-call(bf16[16,448,384]{2,1,0:T(8,128)(2,1)} %all-to-all-done.2.refs_0_.refs_1_.refs_2_.refs_3_, bf16[16,448,384]{2,1,0:T(8,128)(2,1)} %all-to-all-done.2.refs_0_.refs_1_.refs_2_.refs_3_, bf16[16,448,384]{2,1,0:T(8,128)(2,1)} %all-to-all-done.2.refs_0_.refs_1_.refs_2_.refs_3_, ...), custom_call_target="tpu_custom_call" | custom-call | flops 7247757312 | bytes 4718592 | tf_op jit(solution)/shard_map/pallas_call | solution.py:136
  287.6 2.1 pad_maximum_fusion.1
  289.7 17.9 %all-to-all-done.1.x.re_ref.im_ref.mix_ref.tile_ref = bf16[16,160,384]{2,1,0:T(8,128)(2,1)S(1)} async-done(((bf16[16,160,384]{2,1,0:T(8,128)(2,1)}), bf16[16,160,384]{2,1,0:T(8,128)(2,1)S(1)}, u32[]{:S(2)}, u32[]{:S(2)}) %all-to-all-start.1) | async-done | bytes 1966112 | tf_op jit(solution)/shard_map/all_to_all | solution.py:315
  307.5 5.2 %all-to-all-start.3 = ((bf16[16,304,384]{2,1,0:T(8,128)(2,1)}), bf16[16,304,384]{2,1,0:T(8,128)(2,1)}, u32[]{:S(2)}, u32[]{:S(2)}) async-start(bf16[16,304,384]{2,1,0:T(8,128)(2,1)} %pad_maximum_fusion.1), calls=%async_computation.3 | async-start | bytes 7471104 | tf_op jit(solution)/shard_map/all_to_all | solution.py:315
  312.7 0.9 shard_map.29
  314.1 1.2 collective-permute-start.1
  315.8 1.2 collective-permute-start.3
  317.5 2.1 collective-permute-start.5
  319.6 14.5 %collective-permute-done.1.refs_2_ = bf16[48,768]{1,0:T(8,128)(2,1)S(1)} collective-permute-done((bf16[48,768]{1,0:T(8,128)(2,1)S(1)}, bf16[48,768]{1,0:T(8,128)(2,1)S(1)}, u32[]{:S(2)}, u32[]{:S(2)}) %collective-permute-start.1) | collective-permute-done | bytes 73760 | tf_op jit(solution)/shard_map/ppermute | solution.py:308
  334.1 4.4 collective-permute-start.6
  338.6 1.7 copy-done.4
  340.2 10.6 %shard_map.32 = bf16[16,2,48,768]{3,2,1,0:T(8,128)(2,1)S(1)} custom-call(bf16[16,448,384]{2,1,0:T(8,128)(2,1)} %all-to-all-done.2.refs_0_.refs_1_.refs_2_.refs_3_, bf16[16,448,384]{2,1,0:T(8,128)(2,1)} %all-to-all-done.2.refs_0_.refs_1_.refs_2_.refs_3_, bf16[16,448,384]{2,1,0:T(8,128)(2,1)} %all-to-all-done.2.refs_0_.refs_1_.refs_2_.refs_3_, ...), custom_call_target="tpu_custom_call" | custom-call | flops 7247757312 | bytes 4718592 | tf_op jit(solution)/shard_map/pallas_call | solution.py:136
  350.8 1.4 copy-done.2
  352.2 24.6 %collective-permute-done.3.refs_4_ = bf16[48,768]{1,0:T(8,128)(2,1)S(1)} collective-permute-done((bf16[48,768]{1,0:T(8,128)(2,1)S(1)}, bf16[48,768]{1,0:T(8,128)(2,1)S(1)}, u32[]{:S(2)}, u32[]{:S(2)}) %collective-permute-start.3) | collective-permute-done | bytes 73760 | tf_op jit(solution)/shard_map/ppermute | solution.py:308
  376.8 2.4 collective-permute-done.4.refs_5_
  379.3 1.6 collective-permute-done.5.refs_6_
  380.9 1.8 collective-permute-done.6.refs_7_
  382.7 12.4 %all-to-all-done.3.x.re_ref.im_ref.mix_ref.tile_ref = bf16[16,304,384]{2,1,0:T(8,128)(2,1)} async-done(((bf16[16,304,384]{2,1,0:T(8,128)(2,1)}), bf16[16,304,384]{2,1,0:T(8,128)(2,1)}, u32[]{:S(2)}, u32[]{:S(2)}) %all-to-all-start.3) | async-done | bytes 3735584 | tf_op jit(solution)/shard_map/all_to_all | solution.py:315
  395.1 7.8 %all-to-all-start.4 = ((bf16[16,2,48,768]{3,2,1,0:T(8,128)(2,1)}), bf16[16,2,48,768]{3,2,1,0:T(8,128)(2,1)}, u32[]{:S(2)}, u32[]{:S(2)}) async-start(bf16[16,2,48,768]{3,2,1,0:T(8,128)(2,1)} %copy-done.2), calls=%async_computation.4 | async-start | bytes 4718592 | tf_op jit(solution)/shard_map/all_to_all | solution.py:315
  402.9 2.3 shard_map.36
  405.7 1.2 collective-permute-start.15
  407.4 0.7 collective-permute-start.16
  408.1 1.2 collective-permute-start.17
  409.8 2.1 collective-permute-start.19
  411.9 8.9 %collective-permute-done.15.refs_2_ = bf16[48,1536]{1,0:T(8,128)(2,1)S(1)} collective-permute-done((bf16[48,1536]{1,0:T(8,128)(2,1)S(1)}, bf16[48,1536]{1,0:T(8,128)(2,1)S(1)}, u32[]{:S(2)}, u32[]{:S(2)}) %collective-permute-start.15) | collective-permute-done | bytes 147488 | tf_op jit(solution)/shard_map/ppermute | solution.py:308
  420.8 5.2 %collective-permute-start.20 = (bf16[48,1536]{1,0:T(8,128)(2,1)S(1)}, bf16[48,1536]{1,0:T(8,128)(2,1)S(1)}, u32[]{:S(2)}, u32[]{:S(2)}) collective-permute-start(bf16[48,1536]{1,0:T(8,128)(2,1)S(1)} %get-tuple-element.75), channel_id=1, source_target_pairs={{0,7},{1,6},{2,5},{3,4},{4,3},{5,2},{6,1},{7,0},{8,15},{9,14},{10,... | collective-permute-start | bytes 442376 | tf_op jit(solution)/shard_map/ppermute | solution.py:308
  426.6 2.3 shard_map.33
  428.9 1.4 copy-done
  430.3 15.9 %collective-permute-done.17.refs_4_ = bf16[48,1536]{1,0:T(8,128)(2,1)S(1)} collective-permute-done((bf16[48,1536]{1,0:T(8,128)(2,1)S(1)}, bf16[48,1536]{1,0:T(8,128)(2,1)S(1)}, u32[]{:S(2)}, u32[]{:S(2)}) %collective-permute-start.17) | collective-permute-done | bytes 147488 | tf_op jit(solution)/shard_map/ppermute | solution.py:308
  446.3 3.8 collective-permute-done.18.refs_5_
  450.1 3.9 collective-permute-done.19.refs_6_
  454.0 6.1 %collective-permute-done.20.refs_7_ = bf16[48,1536]{1,0:T(8,128)(2,1)S(1)} collective-permute-done((bf16[48,1536]{1,0:T(8,128)(2,1)S(1)}, bf16[48,1536]{1,0:T(8,128)(2,1)S(1)}, u32[]{:S(2)}, u32[]{:S(2)}) %collective-permute-start.20) | collective-permute-done | bytes 147488 | tf_op jit(solution)/shard_map/ppermute | solution.py:308
  460.0 6.5 %shard_map.37 = bf16[32,2,48,768]{3,2,1,0:T(8,128)(2,1)} custom-call(s32[2]{0:T(128)S(1)} %pad_add_fusion.where_ref, bf16[16,304,384]{2,1,0:T(8,128)(2,1)} %all-to-all-done.3.x.re_ref.im_ref.mix_ref.tile_ref, bf16[16,304,384]{2,1,0:T(8,128)(2,1)} %all-to-all-done.3.x.re_ref.im_ref.mix_ref.tile_ref, ...), custom_call_target="tpu_custom_call" | custom-call | bytes 11796480 | tf_op jit(solution)/shard_map/pallas_call | solution.py:281
  466.6 7.3 %pad_maximum_fusion = bf16[64,2,48,768]{3,2,1,0:T(8,128)(2,1)} fusion(bf16[16,2,48,768]{3,2,1,0:T(8,128)(2,1)} %all-to-all-done.4, bf16[32,2,48,768]{3,2,1,0:T(8,128)(2,1)} %shard_map.37, bf16[16,2,48,768]{3,2,1,0:T(8,128)(2,1)S(1)} %copy-done.1), kind=kLoop, calls=%fused_computation.5 | loop fusion | flops 9437184 | bytes 18874368 | tf_op jit(solution)/shard_map/concatenate | solution.py:391
  473.8 21.6 %bitcast_convert_fusion = bf16[48,768,512]{2,1,0:T(8,128)(2,1)} fusion(bf16[64,2,48,768]{3,2,1,0:T(8,128)(2,1)} %pad_maximum_fusion, bf16[64,1,512]{2,0,1:T(8,128)(2,1)S(1)} %fusion.22, bf16[64,1,512]{2,0,1:T(8,128)(2,1)S(1)} %multiply_convert_fusion.1), kind=kOutput, calls=%fused_computation | convolution fusion | flops 4850778112 | bytes 47316992 | tf_op jit(solution)/shard_map/dot_general | solution.py:403
  (33 shorter events, 6.2 us)
Async XLA Ops:
  6.5 41.3 %all-gather.2.cloned.1.call-start = ((), (), s32[]{:S(2)}) async-start(), calls=%async_computation.5 | async-start | bytes 1253376 | tf_op jit(solution)/shard_map/all_gather | solution.py:358
  55.0 78.5 %all-to-all-start = ((bf16[16,2,48,768]{3,2,1,0:T(8,128)(2,1)}), bf16[16,2,48,768]{3,2,1,0:T(8,128)(2,1)S(1)}, u32[]{:S(2)}, u32[]{:S(2)}) async-start(bf16[16,2,48,768]{3,2,1,0:T(8,128)(2,1)} %slice_bitcast_fusion), calls=%async_computation | async-start | bytes 4718592 | tf_op jit(solution)/shard_map/all_to_all | solution.py:315
  66.0 3.9 collective-permute-start.7
  66.4 13.7 %collective-permute-start.8 = (bf16[48,2304]{1,0:T(8,128)(2,1)S(1)}, bf16[48,2304]{1,0:T(8,128)(2,1)S(1)}, u32[]{:S(2)}, u32[]{:S(2)}) collective-permute-start(bf16[48,2304]{1,0:T(8,128)(2,1)S(1)} %get-tuple-element.53), channel_id=1, source_target_pairs={{0,2},{1,3},{2,0},{3,1},{4,6},{5,7},{6,4},{7,5},{8,10},{9,11},{10,... | collective-permute-start | bytes 663560 | tf_op jit(solution)/shard_map/ppermute | solution.py:308
  67.6 18.5 %collective-permute-start.9 = (bf16[48,2304]{1,0:T(8,128)(2,1)S(1)}, bf16[48,2304]{1,0:T(8,128)(2,1)S(1)}, u32[]{:S(2)}, u32[]{:S(2)}) collective-permute-start(bf16[48,2304]{1,0:T(8,128)(2,1)S(1)} %get-tuple-element.54), channel_id=1, source_target_pairs={{0,3},{1,2},{2,1},{3,0},{4,7},{5,6},{6,5},{7,4},{8,11},{9,10},{10,... | collective-permute-start | bytes 663560 | tf_op jit(solution)/shard_map/ppermute | solution.py:308
  68.2 37.5 %collective-permute-start.10 = (bf16[48,2304]{1,0:T(8,128)(2,1)S(1)}, bf16[48,2304]{1,0:T(8,128)(2,1)S(1)}, u32[]{:S(2)}, u32[]{:S(2)}) collective-permute-start(bf16[48,2304]{1,0:T(8,128)(2,1)S(1)} %get-tuple-element.55), channel_id=1, source_target_pairs={{0,4},{1,5},{2,6},{3,7},{4,0},{5,1},{6,2},{7,3},{8,12},{9,13},{10,... | collective-permute-start | bytes 663560 | tf_op jit(solution)/shard_map/ppermute | solution.py:308
  69.4 42.0 %collective-permute-start.11 = (bf16[48,2304]{1,0:T(8,128)(2,1)S(1)}, bf16[48,2304]{1,0:T(8,128)(2,1)S(1)}, u32[]{:S(2)}, u32[]{:S(2)}) collective-permute-start(bf16[48,2304]{1,0:T(8,128)(2,1)S(1)} %get-tuple-element.56), channel_id=1, source_target_pairs={{0,5},{1,4},{2,7},{3,6},{4,1},{5,0},{6,3},{7,2},{8,13},{9,12},{10,... | collective-permute-start | bytes 663560 | tf_op jit(solution)/shard_map/ppermute | solution.py:308
  69.9 48.2 %collective-permute-start.12 = (bf16[48,2304]{1,0:T(8,128)(2,1)S(1)}, bf16[48,2304]{1,0:T(8,128)(2,1)S(1)}, u32[]{:S(2)}, u32[]{:S(2)}) collective-permute-start(bf16[48,2304]{1,0:T(8,128)(2,1)S(1)} %get-tuple-element.57), channel_id=1, source_target_pairs={{0,6},{1,7},{2,4},{3,5},{4,2},{5,3},{6,0},{7,1},{8,14},{9,15},{10,... | collective-permute-start | bytes 663560 | tf_op jit(solution)/shard_map/ppermute | solution.py:308
  80.2 42.9 %collective-permute-start.13 = (bf16[48,2304]{1,0:T(8,128)(2,1)S(1)}, bf16[48,2304]{1,0:T(8,128)(2,1)S(1)}, u32[]{:S(2)}, u32[]{:S(2)}) collective-permute-start(bf16[48,2304]{1,0:T(8,128)(2,1)S(1)} %get-tuple-element.58), channel_id=1, source_target_pairs={{0,7},{1,6},{2,5},{3,4},{4,3},{5,2},{6,1},{7,0},{8,15},{9,14},{10,... | collective-permute-start | bytes 663560 | tf_op jit(solution)/shard_map/ppermute | solution.py:308
  133.4 124.5 %all-to-all-start.2 = ((bf16[16,448,384]{2,1,0:T(8,128)(2,1)}), bf16[16,448,384]{2,1,0:T(8,128)(2,1)}, u32[]{:S(2)}, u32[]{:S(2)}) async-start(bf16[16,448,384]{2,1,0:T(8,128)(2,1)} %shard_map.31), calls=%async_computation.2 | async-start | bytes 11010048 | tf_op jit(solution)/shard_map/all_to_all | solution.py:315
  148.3 1.3 copy-start.5
  258.0 49.6 %all-to-all-start.1 = ((bf16[16,160,384]{2,1,0:T(8,128)(2,1)}), bf16[16,160,384]{2,1,0:T(8,128)(2,1)S(1)}, u32[]{:S(2)}, u32[]{:S(2)}) async-start(bf16[16,160,384]{2,1,0:T(8,128)(2,1)} %copy-done.5), calls=%async_computation.1 | async-start | bytes 3932160 | tf_op jit(solution)/shard_map/all_to_all | solution.py:315
  263.6 1.7 copy-start.3
  307.5 87.5 %all-to-all-start.3 = ((bf16[16,304,384]{2,1,0:T(8,128)(2,1)}), bf16[16,304,384]{2,1,0:T(8,128)(2,1)}, u32[]{:S(2)}, u32[]{:S(2)}) async-start(bf16[16,304,384]{2,1,0:T(8,128)(2,1)} %pad_maximum_fusion.1), calls=%async_computation.3 | async-start | bytes 7471104 | tf_op jit(solution)/shard_map/all_to_all | solution.py:315
  313.6 3.9 collective-permute-start
  314.1 20.1 %collective-permute-start.1 = (bf16[48,768]{1,0:T(8,128)(2,1)S(1)}, bf16[48,768]{1,0:T(8,128)(2,1)S(1)}, u32[]{:S(2)}, u32[]{:S(2)}) collective-permute-start(bf16[48,768]{1,0:T(8,128)(2,1)S(1)} %get-tuple-element.45), channel_id=1, source_target_pairs={{0,2},{1,3},{2,0},{3,1},{4,6},{5,7},{6,4},{7,5},{8,10},{9,11},{10,... | collective-permute-start | bytes 221192 | tf_op jit(solution)/shard_map/ppermute | solution.py:308
  315.2 37.0 %collective-permute-start.2 = (bf16[48,768]{1,0:T(8,128)(2,1)S(1)}, bf16[48,768]{1,0:T(8,128)(2,1)S(1)}, u32[]{:S(2)}, u32[]{:S(2)}) collective-permute-start(bf16[48,768]{1,0:T(8,128)(2,1)S(1)} %get-tuple-element.46), channel_id=1, source_target_pairs={{0,3},{1,2},{2,1},{3,0},{4,7},{5,6},{6,5},{7,4},{8,11},{9,10},{10,... | collective-permute-start | bytes 221192 | tf_op jit(solution)/shard_map/ppermute | solution.py:308
  315.8 61.0 %collective-permute-start.3 = (bf16[48,768]{1,0:T(8,128)(2,1)S(1)}, bf16[48,768]{1,0:T(8,128)(2,1)S(1)}, u32[]{:S(2)}, u32[]{:S(2)}) collective-permute-start(bf16[48,768]{1,0:T(8,128)(2,1)S(1)} %get-tuple-element.47), channel_id=1, source_target_pairs={{0,4},{1,5},{2,6},{3,7},{4,0},{5,1},{6,2},{7,3},{8,12},{9,13},{10,... | collective-permute-start | bytes 221192 | tf_op jit(solution)/shard_map/ppermute | solution.py:308
  317.0 62.2 %collective-permute-start.4 = (bf16[48,768]{1,0:T(8,128)(2,1)S(1)}, bf16[48,768]{1,0:T(8,128)(2,1)S(1)}, u32[]{:S(2)}, u32[]{:S(2)}) collective-permute-start(bf16[48,768]{1,0:T(8,128)(2,1)S(1)} %get-tuple-element.48), channel_id=1, source_target_pairs={{0,5},{1,4},{2,7},{3,6},{4,1},{5,0},{6,3},{7,2},{8,13},{9,12},{10,... | collective-permute-start | bytes 221192 | tf_op jit(solution)/shard_map/ppermute | solution.py:308
  317.5 63.3 %collective-permute-start.5 = (bf16[48,768]{1,0:T(8,128)(2,1)S(1)}, bf16[48,768]{1,0:T(8,128)(2,1)S(1)}, u32[]{:S(2)}, u32[]{:S(2)}) collective-permute-start(bf16[48,768]{1,0:T(8,128)(2,1)S(1)} %get-tuple-element.49), channel_id=1, source_target_pairs={{0,6},{1,7},{2,4},{3,5},{4,2},{5,3},{6,0},{7,1},{8,14},{9,15},{10,... | collective-permute-start | bytes 221192 | tf_op jit(solution)/shard_map/ppermute | solution.py:308
  334.1 48.5 %collective-permute-start.6 = (bf16[48,768]{1,0:T(8,128)(2,1)S(1)}, bf16[48,768]{1,0:T(8,128)(2,1)S(1)}, u32[]{:S(2)}, u32[]{:S(2)}) collective-permute-start(bf16[48,768]{1,0:T(8,128)(2,1)S(1)} %get-tuple-element.50), channel_id=1, source_target_pairs={{0,7},{1,6},{2,5},{3,4},{4,3},{5,2},{6,1},{7,0},{8,15},{9,14},{10,... | collective-permute-start | bytes 221192 | tf_op jit(solution)/shard_map/ppermute | solution.py:308
  338.6 1.7 copy-start.4
  350.8 1.4 copy-start.2
  395.1 71.5 %all-to-all-start.4 = ((bf16[16,2,48,768]{3,2,1,0:T(8,128)(2,1)}), bf16[16,2,48,768]{3,2,1,0:T(8,128)(2,1)}, u32[]{:S(2)}, u32[]{:S(2)}) async-start(bf16[16,2,48,768]{3,2,1,0:T(8,128)(2,1)} %copy-done.2), calls=%async_computation.4 | async-start | bytes 4718592 | tf_op jit(solution)/shard_map/all_to_all | solution.py:315
  405.3 4.6 collective-permute-start.14
  405.7 15.2 %collective-permute-start.15 = (bf16[48,1536]{1,0:T(8,128)(2,1)S(1)}, bf16[48,1536]{1,0:T(8,128)(2,1)S(1)}, u32[]{:S(2)}, u32[]{:S(2)}) collective-permute-start(bf16[48,1536]{1,0:T(8,128)(2,1)S(1)} %get-tuple-element.70), channel_id=1, source_target_pairs={{0,2},{1,3},{2,0},{3,1},{4,6},{5,7},{6,4},{7,5},{8,10},{9,11},{10,... | collective-permute-start | bytes 442376 | tf_op jit(solution)/shard_map/ppermute | solution.py:308
  407.4 22.9 %collective-permute-start.16 = (bf16[48,1536]{1,0:T(8,128)(2,1)S(1)}, bf16[48,1536]{1,0:T(8,128)(2,1)S(1)}, u32[]{:S(2)}, u32[]{:S(2)}) collective-permute-start(bf16[48,1536]{1,0:T(8,128)(2,1)S(1)} %get-tuple-element.71), channel_id=1, source_target_pairs={{0,3},{1,2},{2,1},{3,0},{4,7},{5,6},{6,5},{7,4},{8,11},{9,10},{10,... | collective-permute-start | bytes 442376 | tf_op jit(solution)/shard_map/ppermute | solution.py:308
  408.1 38.1 %collective-permute-start.17 = (bf16[48,1536]{1,0:T(8,128)(2,1)S(1)}, bf16[48,1536]{1,0:T(8,128)(2,1)S(1)}, u32[]{:S(2)}, u32[]{:S(2)}) collective-permute-start(bf16[48,1536]{1,0:T(8,128)(2,1)S(1)} %get-tuple-element.72), channel_id=1, source_target_pairs={{0,4},{1,5},{2,6},{3,7},{4,0},{5,1},{6,2},{7,3},{8,12},{9,13},{10,... | collective-permute-start | bytes 442376 | tf_op jit(solution)/shard_map/ppermute | solution.py:308
  409.3 40.8 %collective-permute-start.18 = (bf16[48,1536]{1,0:T(8,128)(2,1)S(1)}, bf16[48,1536]{1,0:T(8,128)(2,1)S(1)}, u32[]{:S(2)}, u32[]{:S(2)}) collective-permute-start(bf16[48,1536]{1,0:T(8,128)(2,1)S(1)} %get-tuple-element.73), channel_id=1, source_target_pairs={{0,5},{1,4},{2,7},{3,6},{4,1},{5,0},{6,3},{7,2},{8,13},{9,12},{10,... | collective-permute-start | bytes 442376 | tf_op jit(solution)/shard_map/ppermute | solution.py:308
  409.8 44.2 %collective-permute-start.19 = (bf16[48,1536]{1,0:T(8,128)(2,1)S(1)}, bf16[48,1536]{1,0:T(8,128)(2,1)S(1)}, u32[]{:S(2)}, u32[]{:S(2)}) collective-permute-start(bf16[48,1536]{1,0:T(8,128)(2,1)S(1)} %get-tuple-element.74), channel_id=1, source_target_pairs={{0,6},{1,7},{2,4},{3,5},{4,2},{5,3},{6,0},{7,1},{8,14},{9,15},{10,... | collective-permute-start | bytes 442376 | tf_op jit(solution)/shard_map/ppermute | solution.py:308
  420.8 39.2 %collective-permute-start.20 = (bf16[48,1536]{1,0:T(8,128)(2,1)S(1)}, bf16[48,1536]{1,0:T(8,128)(2,1)S(1)}, u32[]{:S(2)}, u32[]{:S(2)}) collective-permute-start(bf16[48,1536]{1,0:T(8,128)(2,1)S(1)} %get-tuple-element.75), channel_id=1, source_target_pairs={{0,7},{1,6},{2,5},{3,4},{4,3},{5,2},{6,1},{7,0},{8,15},{9,14},{10,... | collective-permute-start | bytes 442376 | tf_op jit(solution)/shard_map/ppermute | solution.py:308
  428.9 1.4 copy-start
  460.0 6.5 %copy-start.1 = (bf16[16,2,48,768]{3,2,1,0:T(8,128)(2,1)S(1)}, bf16[16,2,48,768]{3,2,1,0:T(8,128)(2,1)}, u32[]{:S(2)}) copy-start(bf16[16,2,48,768]{3,2,1,0:T(8,128)(2,1)} %copy-done) | copy-start | bytes 7077892
Sparse Core Ops, SparseCore 0:
  9.6 38.1 all-gather.1

commit v3 on v2

--- a/solution.py
+++ b/solution.py
@@ -44,7 +44,7 @@
     return kept(s // rows, r // rows, s, r, group), s == r
 
 
-def chain_kernel(rows, slot, packed_in, packed_out, *refs):
+def chain_kernel(rows, slot_in, slot_out, packed_in, packed_out, *refs):
     count = 4 if packed_in else 1
     ins, ratio, out, (br, bi, fr, fi) = refs[:count], refs[count], refs[count + 1], refs[count + 2 :]
     order = br.shape[0]
@@ -68,14 +68,14 @@
             tr = jnp.where(mask, 0.0, both)
             br[pick, pick] = ((tr + tr.T) * ratio[pick, pick]).astype(b16)
             line = jnp.sum(
-                extra[h * (n // 2) : (h + 1) * (n // 2), slot : slot + 1].astype(f32), axis=0
+                extra[h * (n // 2) : (h + 1) * (n // 2), slot_in : slot_in + 1].astype(f32), axis=0
             )
             ti = jnp.where(mask, both, 0.0)
             ti = ti + ti.T + jnp.where(diag, 2.0 * line, 0.0)
             bi[pick, pick] = (ti * ratio[pick, pick]).astype(b16)
     else:
         for c, b in ((0, br), (1, bi)):
-            y = ins[0][:, c].reshape(order, order).astype(f32)
+            y = ins[0][:, 0, c].reshape(order, order).astype(f32)
             b[...] = ((y + y.T) * ratio[...]).astype(b16)
     step = 256 if order % 256 == 0 else order
     for t in range(0, order, step):
@@ -106,7 +106,7 @@
             out[dst, 2 * rows : 3 * rows] = jnp.where(mask, pi, pr).astype(b16).reshape(shape)
             line = jnp.sum(jnp.where(diag, pi, 0.0), axis=0, keepdims=True)
             tile = jnp.where(
-                lax.broadcasted_iota(jnp.int32, (TILE, half), 0) == slot,
+                lax.broadcasted_iota(jnp.int32, (TILE, half), 0) == slot_out,
                 jnp.broadcast_to(line, (TILE, half)),
                 0.0,
             ).astype(b16)
@@ -119,7 +119,6 @@
 def chain(got, ratio, rows, order, slot_in, total_in, slot_out, packed_out):
     n, half = order // rows, order // 2
     packed_in = total_in > 0
-    slot = slot_in if packed_in else slot_out
     if packed_in:
         specs = [
             pl.BlockSpec((n, rows, half), functools.partial(lambda b, i: (0, b, 0), 3 * slot_in + c))
@@ -129,12 +128,12 @@
         specs.append(pl.BlockSpec((n, TILE, half), lambda i: (0, last, 0)))
         args = [got] * 4 + [ratio]
     else:
-        specs = [pl.BlockSpec((n, 2, rows, order), lambda i: (0, 0, 0, 0))]
+        specs = [pl.BlockSpec((n, 1, 2, rows, order), lambda i: (0, slot_in, 0, 0, 0))]
         args = [got, ratio]
     specs.append(pl.BlockSpec((order, order), lambda i: (0, 0)))
     shape = (n, 3 * rows + TILE, half) if packed_out else (n, 2, rows, order)
     return pl.pallas_call(
-        functools.partial(chain_kernel, rows, slot, packed_in, packed_out),
+        functools.partial(chain_kernel, rows, slot_in, slot_out, packed_in, packed_out),
         out_shape=jax.ShapeDtypeStruct(shape, jnp.bfloat16),
         grid=(1,),
         in_specs=specs,
@@ -152,6 +151,94 @@
     )(*args)
 
 
+def dft_kernel(first, table, weight, traces, head, tail, turn):
+    rb, cb = traces.shape[:2]
+    count = table.shape[0]
+    b16 = jnp.bfloat16
+    for s in range(rb):
+        lines = lax.dot_general(
+            traces[s], table[...], (((1,), (1,)), ((), ())), preferred_element_type=jnp.float32
+        ).T
+        lines = lines * weight[s : s + 1]
+        for c in range(cb // 128):
+            turn[c, pl.ds(s, count, stride=rb), :] = lines[:, c * 128 : (c + 1) * 128]
+    for c in range(cb // 128):
+        pick = slice(c * 128, (c + 1) * 128)
+        head[:, :, pick] = turn[c, : first * rb].reshape(first, rb, 128).astype(b16)
+        tail[:, :, pick] = turn[c, first * rb :].reshape(count - first, rb, 128).astype(b16)
+
+
+def dft(traces, weight, table, first):
+    rows, order, nt = traces.shape
+    count = table.shape[0]
+    rb, cb = 16, 384 if order % 384 == 0 else 128
+    return pl.pallas_call(
+        functools.partial(dft_kernel, first),
+        out_shape=[
+            jax.ShapeDtypeStruct((first, rows, order), jnp.bfloat16),
+            jax.ShapeDtypeStruct((count - first, rows, order), jnp.bfloat16),
+        ],
+        grid=(rows // rb, order // cb),
+        in_specs=[
+            pl.BlockSpec((count, nt), lambda i, j: (0, 0)),
+            pl.BlockSpec((rb, cb), lambda i, j: (i, j)),
+            pl.BlockSpec((rb, cb, nt), lambda i, j: (i, j, 0)),
+        ],
+        out_specs=[
+            pl.BlockSpec((first, rb, cb), lambda i, j: (0, i, j)),
+            pl.BlockSpec((count - first, rb, cb), lambda i, j: (0, i, j)),
+        ],
+        scratch_shapes=[pltpu.VMEM((cb // 128, count * rb, 128), jnp.float32)],
+        compiler_params=pltpu.CompilerParams(vmem_limit_bytes=52 * 1024 * 1024),
+        cost_estimate=pl.CostEstimate(
+            flops=4 * count * rows * order * nt,
+            bytes_accessed=2 * rows * order * (nt + count),
+            transcendentals=0,
+        ),
+    )(table, weight, traces)
+
+
+def idft_kernel(parts, table, *refs):
+    ins, out, turn = refs[:parts], refs[parts], refs[parts + 1]
+    rb, cb = out.shape[:2]
+    count = table.shape[0]
+    at = 0
+    for ref in ins:
+        size = ref.shape[0] * rb
+        for c in range(cb // 128):
+            piece = ref[:, :, c * 128 : (c + 1) * 128].astype(jnp.float32)
+            turn[c, at : at + size] = piece.reshape(size, 128)
+        at += size
+    for s in range(rb):
+        for c in range(cb // 128):
+            lines = turn[c, pl.ds(s, count, stride=rb), :].astype(jnp.bfloat16)
+            samples = lax.dot_general(
+                lines, table[...], (((0,), (0,)), ((), ())), preferred_element_type=jnp.float32
+            )
+            out[s, c * 128 : (c + 1) * 128] = samples.astype(jnp.bfloat16)
+
+
+def idft(pieces, table):
+    count, nt = table.shape
+    rows, order = pieces[0].shape[1:]
+    rb, cb = 16, 384 if order % 384 == 0 else 128
+    return pl.pallas_call(
+        functools.partial(idft_kernel, len(pieces)),
+        out_shape=jax.ShapeDtypeStruct((rows, order, nt), jnp.bfloat16),
+        grid=(rows // rb, order // cb),
+        in_specs=[pl.BlockSpec((count, nt), lambda i, j: (0, 0))]
+        + [pl.BlockSpec((piece.shape[0], rb, cb), lambda i, j: (0, i, j)) for piece in pieces],
+        out_specs=pl.BlockSpec((rb, cb, nt), lambda i, j: (i, j, 0)),
+        scratch_shapes=[pltpu.VMEM((cb // 128, count * rb, 128), jnp.float32)],
+        compiler_params=pltpu.CompilerParams(vmem_limit_bytes=52 * 1024 * 1024),
+        cost_estimate=pl.CostEstimate(
+            flops=4 * count * rows * order * nt,
+            bytes_accessed=2 * rows * order * (nt + count),
+            transcendentals=0,
+        ),
+    )(table, *pieces)
+
+
 def side(ref, upper, inside):
     half = ref.shape[-1] // 2
     low, high = ref[..., :half].astype(jnp.float32), ref[..., half:].astype(jnp.float32)
@@ -164,7 +251,7 @@
     n, half = 2 * group, rows * group
     if whole:
         mask, diag = pair_mask(rows, group, me * rows, rows)
-        re, im = side(x.at[:, 0, 0], upper, True), side(x.at[:, 0, 1], upper, True)
+        re, im = side(x.at[0, :, 0], upper, True), side(x.at[0, :, 1], upper, True)
         block = jnp.where(diag[None], 0.0, jnp.where(mask[None], re, im))
     else:
         block = x[...].astype(jnp.float32)
@@ -173,10 +260,10 @@
         outs[m][...] = turned[me ^ m]
 
 
-def give(x, where, rows, group, count, whole):
+def give(x, where, rows, group, first, count, whole):
     n, half = 2 * group, rows * group
     if whole:
-        spec = pl.BlockSpec((n, 1, 2, rows, 2 * half), lambda f, w: (0, f + 1, 0, 0, 0))
+        spec = pl.BlockSpec((1, n, 2, rows, 2 * half), lambda f, w: (f + first, 0, 0, 0, 0))
     else:
         spec = pl.BlockSpec((n, rows, half), lambda f, w: (0, 3 * f + 2, 0))
     return pl.pallas_call(
@@ -214,8 +301,8 @@
     mask, diag = pair_mask(rows, group, me * rows, rows)
     base = pl.multiple_of(f * 3 * rows, 16)
     for c in range(2):
-        out[:, pl.ds(base + c * rows, rows)] = side(x.at[:, 0, c], upper, False).astype(b16)
-    re, im = side(x.at[:, 0, 0], upper, True), side(x.at[:, 0, 1], upper, True)
+        out[:, pl.ds(base + c * rows, rows)] = side(x.at[0, :, c], upper, False).astype(b16)
+    re, im = side(x.at[0, :, 0], upper, True), side(x.at[0, :, 1], upper, True)
     keep = jnp.where(mask[None], im, re) + other[...]
     out[:, pl.ds(base + 2 * rows, rows)] = keep.astype(b16)
     line = jnp.sum(jnp.where(diag[None], im, 0.0), axis=1, keepdims=True)
@@ -230,7 +317,7 @@
     out[:, count * 3 * rows :] = (old + tile).astype(b16)
 
 
-def pack(x, pieces, where, rows, group, count):
+def pack(x, pieces, where, rows, group, first, count):
     n, half = 2 * group, rows * group
     shape = (n, count * 3 * rows + TILE, half)
     return pl.pallas_call(
@@ -239,7 +326,7 @@
         grid_spec=pltpu.PrefetchScalarGridSpec(
             num_scalar_prefetch=1,
             grid=(count,),
-            in_specs=[pl.BlockSpec((n, 1, 2, rows, 2 * half), lambda f, w: (0, f + 1, 0, 0, 0))]
+            in_specs=[pl.BlockSpec((1, n, 2, rows, 2 * half), lambda f, w: (f + first, 0, 0, 0, 0))]
             + [pl.BlockSpec((rows, n * rows), lambda f, w: (0, f))] * group,
             out_specs=pl.BlockSpec(shape, lambda f, w: (0, 0, 0)),
             scratch_shapes=[
@@ -355,40 +442,40 @@
     index = lax.axis_index("tile")
     where = jnp.stack([index % group, (index < group).astype(jnp.int32)])
 
-    every = lax.all_gather(weight.astype(b16), "tile", axis=0, tiled=True).astype(jnp.float32)
+    every = lax.all_gather(weight.astype(b16), "tile", axis=0, tiled=True)
+    lead = per // 2
+    rest = per - lead
+    table = forward.reshape(per, n, 2, NT)
+    flat = (-1, NT)
+    table_in = jnp.concatenate(
+        [table[:lead].transpose(1, 0, 2, 3).reshape(flat), table[lead:].reshape(flat)], 0
+    )
+    table_out = jnp.concatenate(
+        [table[:lead].reshape(flat), table[lead:].transpose(1, 0, 2, 3).reshape(flat)], 0
+    )
+    head, tail = dft(traces, weight, table_in, 2 * lead * n)
+    tail = tail.reshape(rest, n, 2, rows, order)
+    gifts = give(tail, where, rows, group, 0, rest, True)
+    head, gifts = lax.optimization_barrier((head, gifts))
+    whole = a2a(head.reshape(n, lead, 2, rows, order))
+    packed = pack(tail, swap(gifts, n), where, rows, group, 0, rest)
+    packed, every = lax.optimization_barrier((packed, every))
+    every = every.astype(jnp.float32)
     ratio = 1.0 / (every + every.T)
-    part = forward.reshape(per, n, 2, NT).transpose(1, 0, 2, 3)
-    mixed = (weight * spectrum_of(part, traces)).astype(b16)
-    mixed, ratio = lax.optimization_barrier((mixed, ratio))
-
-    whole = a2a(mixed[:, 0])
-    rest = per - 1
-    pieces = swap(give(mixed, where, rows, group, rest, True), n)
-    got = a2a(pack(mixed, pieces, where, rows, group, rest))
-
-    answers = [chain(whole, ratio, rows, order, 0, 0, 0, True)]
-    for f in range(rest):
-        answers.append(chain(got, ratio, rows, order, f, rest, f, f < rest - 1))
-
-    def bring(fs):
-        count = len(fs)
-        if count > 1:
-            tile = sum(answers[f][:, 3 * rows :] for f in fs)
-            sent = jnp.concatenate([answers[f][:, : 3 * rows] for f in fs] + [tile], 1)
-        else:
-            sent = answers[fs[0]]
-        back = a2a(sent)
-        return back, swap(give(back, where, rows, group, count, False), n)
-
-    early = bring([0])
-    later = bring(list(range(1, per - 1)))
-    early, final = lax.optimization_barrier((early, answers[-1]))
-    returned = [
-        unpack(*early, where, rows, group, 1),
-        unpack(*later, where, rows, group, per - 2),
-        a2a(final),
-    ]
-    return jnp.concatenate(returned, 0)
+    got = a2a(packed)
+
+    parts = [chain(whole, ratio, rows, order, f, 0, f, True) for f in range(lead)]
+    tile = sum(part[:, 3 * rows :] for part in parts)
+    back = jnp.concatenate([part[:, : 3 * rows] for part in parts] + [tile], 1)
+    back, got = lax.optimization_barrier((back, got))
+    back = a2a(back)
+    parts = [chain(got, ratio, rows, order, f, rest, 0, False) for f in range(rest)]
+    parts = jnp.stack(parts, 1)
+    gifts = give(back, where, rows, group, 0, lead, False)
+    parts, gifts = lax.optimization_barrier((parts, gifts))
+    last = a2a(parts)
+    full = unpack(back, swap(gifts, n), where, rows, group, lead)
+    return idft([part.reshape(-1, rows, order) for part in (full, last)], table_out)
 
 
 def body(traces, quality):
@@ -396,10 +483,9 @@
     n = order // rows
     forward = tables()
     weight = (quality + 1).astype(jnp.float32)
-    if rows % 16 == 0 and order % 256 == 0 and n & (n - 1) == 0 and NF // n >= 3:
-        returned = pipelined(traces, weight, forward, n)
-    else:
-        returned = generic(traces, weight, forward, n)
+    if rows % 16 == 0 and order % 256 == 0 and n & (n - 1) == 0 and NF // n >= 4:
+        return pipelined(traces, weight, forward, n)
+    returned = generic(traces, weight, forward, n)
     result = lax.dot_general(
         returned, forward, (((0, 1), (0, 1)), ((), ())), preferred_element_type=jnp.float32
     )

time: 511 us -> 483 us (0.945)
  the two profiles are of different devices: /device:TPU:17 before, /device:TPU:15 now
where the time goes in v3:
time: 483 us; the launch traced here: 474 us
  waiting for transfers between devices  293 us (61%)
  Pallas kernels  98 us (20%)
  starting transfers between devices  45.9 us (10%)
  between operations  13.9 us (3%)
  local copies, waits for them, and re-layouts  13.3 us (3%)
  other arithmetic  9.49 us (2%)
    ppermute x14, waiting for transfers between devices, swap(): lax.ppermute(piece, 'tile', [(i, i ^ m) for i in range(n)])  166 us
    all_to_all x4, waiting for transfers between devices, a2a(): return lax.all_to_all(x, 'tile', split_axis=0, concat_axis=0, tiled=True)  127 us
    pallas_call x4, Pallas kernels, chain(): pl.pallas_call(functools.partial(chain_kernel, rows, slot_in, slot_out, p...  41.9 us
    all_to_all x4, starting transfers between devices, a2a(): return lax.all_to_all(x, 'tile', split_axis=0, concat_axis=0, tiled=True)  25.5 us
    pallas_call x1, Pallas kernels, dft(): pl.pallas_call(functools.partial(dft_kernel, first), out_shape=[jax.Shape...  20.5 us
    ppermute x14, starting transfers between devices, swap(): lax.ppermute(piece, 'tile', [(i, i ^ m) for i in range(n)])  20.4 us
    pallas_call x1, Pallas kernels, idft(): pl.pallas_call(functools.partial(idft_kernel, len(pieces)), out_shape=jax...  18.9 us
  transfers between devices with their start and end apart: 19, of which 15 were waited for; matrix products, arithmetic and copies ran while one was open for 2% of the time, Pallas kernels for 11%

profile of v3, /device:TPU:15, one launch (start us, length us, event | category | flops | bytes accessed | tf_op | source)
XLA Modules:
  0.0 473.6 jit_solution(11605292491623000178)
XLA Ops:
  6.5 0.6 fusion.7
  7.1 0.6 multiply_convert_fusion.1
  7.7 0.6 copy-done.5
  8.3 0.1 copy.24
  8.4 0.1 copy.19
  8.6 1.6 fusion.9
  10.1 0.1 pad_add_fusion.where_ref
  10.2 20.5 %shard_map.28 = (bf16[64,48,768]{2,1,0:T(8,128)(2,1)}, bf16[64,48,768]{2,1,0:T(8,128)(2,1)}) custom-call(bf16[128,512]{1,0:T(8,128)(2,1)S(1)} %pad_maximum_fusion.3.table, f32[48,768]{1,0:T(8,128)S(1)} %get-tuple-element.86.weight, bf16[48,768,512]{2,1,0:T(8,128)(2,1)} %traces.1), custom_call_target="tpu_custom_call" | custom-call | flops 9663676416 | bytes 47185920 | tf_op jit(solution)/shard_map/pallas_call | solution.py:175
  30.7 2.3 copy-done
  33.0 1.9 shard_map.29
  35.0 6.6 %all-to-all-start = ((bf16[16,2,2,48,768]{4,3,2,1,0:T(8,128)(2,1)}), bf16[16,2,2,48,768]{4,3,2,1,0:T(8,128)(2,1)}, u32[]{:S(2)}, u32[]{:S(2)}) async-start(bf16[16,2,2,48,768]{4,3,2,1,0:T(8,128)(2,1)} %bitcast.24), calls=%async_computation | async-start | bytes 9437184 | tf_op jit(solution)/shard_map/all_to_all | solution.py:402
  41.5 0.0 all-gather.2.cloned.1.call-start
  41.6 0.7 all-gather.2.cloned.1.call-update
  42.3 0.4 collective-permute-start
  42.7 0.3 collective-permute-start.1
  43.0 1.5 collective-permute-start.2
  44.5 0.3 collective-permute-start.3
  44.8 1.4 collective-permute-start.4
  46.2 0.1 collective-permute-start.5
  46.2 19.8 %collective-permute-done.1.refs_2_ = bf16[48,1536]{1,0:T(8,128)(2,1)S(1)} collective-permute-done((bf16[48,1536]{1,0:T(8,128)(2,1)S(1)}, bf16[48,1536]{1,0:T(8,128)(2,1)S(1)}, u32[]{:S(2)}, u32[]{:S(2)}) %collective-permute-start.1) | collective-permute-done | bytes 147488 | tf_op jit(solution)/shard_map/ppermute | solution.py:395
  66.0 9.1 %collective-permute-start.6 = (bf16[48,1536]{1,0:T(8,128)(2,1)S(1)}, bf16[48,1536]{1,0:T(8,128)(2,1)S(1)}, u32[]{:S(2)}, u32[]{:S(2)}) collective-permute-start(bf16[48,1536]{1,0:T(8,128)(2,1)S(1)} %get-tuple-element.63), channel_id=1, source_target_pairs={{0,7},{1,6},{2,5},{3,4},{4,3},{5,2},{6,1},{7,0},{8,15},{9,14},{10,... | collective-permute-start | bytes 442376 | tf_op jit(solution)/shard_map/ppermute | solution.py:395
  75.1 0.3 collective-permute-done.2.refs_3_
  75.3 54.5 %collective-permute-done.3.refs_4_ = bf16[48,1536]{1,0:T(8,128)(2,1)S(1)} collective-permute-done((bf16[48,1536]{1,0:T(8,128)(2,1)S(1)}, bf16[48,1536]{1,0:T(8,128)(2,1)S(1)}, u32[]{:S(2)}, u32[]{:S(2)}) %collective-permute-start.3) | collective-permute-done | bytes 147488 | tf_op jit(solution)/shard_map/ppermute | solution.py:395
  129.9 4.1 collective-permute-done.4.refs_5_
  134.0 1.4 collective-permute-done.5.refs_6_
  135.4 3.2 collective-permute-done.6.refs_7_
  138.5 6.0 %shard_map.30 = bf16[16,304,384]{2,1,0:T(8,128)(2,1)S(1)} custom-call(s32[2]{0:T(128)S(1)} %pad_add_fusion.where_ref, bf16[2,16,2,48,768]{4,3,2,1,0:T(8,128)(2,1)} %bitcast.19, bf16[48,1536]{1,0:T(8,128)(2,1)S(1)} %get-tuple-element.56.refs_0_, bf16[48,1536]{1,0:T(8,128)(2,1)S(1)} %collective-permute-done.refs_1_, ...), custom_call_target="tpu_custom_call" | custom-call | bytes 11796480 | tf_op jit(solution)/shard_map/pallas_call | solution.py:323
  144.5 1.8 copy-done.1
  146.3 6.0 %all-to-all-done.refs_0_ = bf16[16,2,2,48,768]{4,3,2,1,0:T(8,128)(2,1)} async-done(((bf16[16,2,2,48,768]{4,3,2,1,0:T(8,128)(2,1)}), bf16[16,2,2,48,768]{4,3,2,1,0:T(8,128)(2,1)}, u32[]{:S(2)}, u32[]{:S(2)}) %all-to-all-start) | async-done | bytes 4718624 | tf_op jit(solution)/shard_map/all_to_all | solution.py:402
  152.3 9.0 %all-to-all-start.1 = ((bf16[16,304,384]{2,1,0:T(8,128)(2,1)}), bf16[16,304,384]{2,1,0:T(8,128)(2,1)}, u32[]{:S(2)}, u32[]{:S(2)}) async-start(bf16[16,304,384]{2,1,0:T(8,128)(2,1)} %copy-done.1), calls=%async_computation.1 | async-start | bytes 7471104 | tf_op jit(solution)/shard_map/all_to_all | solution.py:402
  161.3 0.6 copy.20
  162.0 2.2 copy.21
  164.2 2.1 fusion.refs_1_.refs_4_
  166.3 10.2 %shard_map.31 = bf16[16,160,384]{2,1,0:T(8,128)(2,1)S(1)} custom-call(bf16[16,2,2,48,768]{4,3,2,1,0:T(8,128)(2,1)} %all-to-all-done.refs_0_, f32[768,768]{1,0:T(8,128)S(1)} %fusion.refs_1_.refs_4_), custom_call_target="tpu_custom_call" | custom-call | flops 7247757312 | bytes 4718592 | tf_op jit(solution)/shard_map/pallas_call | solution.py:135
  176.5 0.2 slice.36
  176.6 10.4 %shard_map.32 = bf16[16,160,384]{2,1,0:T(8,128)(2,1)S(1)} custom-call(bf16[16,2,2,48,768]{4,3,2,1,0:T(8,128)(2,1)} %all-to-all-done.refs_0_, f32[768,768]{1,0:T(8,128)S(1)} %fusion.refs_1_.refs_4_), custom_call_target="tpu_custom_call" | custom-call | flops 7247757312 | bytes 4718592 | tf_op jit(solution)/shard_map/pallas_call | solution.py:135
  187.0 0.2 slice.37
  187.2 2.0 pad_maximum_fusion.1
  189.2 54.7 %all-to-all-done.1.refs_0_.refs_1_.refs_2_.refs_3_ = bf16[16,304,384]{2,1,0:T(8,128)(2,1)} async-done(((bf16[16,304,384]{2,1,0:T(8,128)(2,1)}), bf16[16,304,384]{2,1,0:T(8,128)(2,1)}, u32[]{:S(2)}, u32[]{:S(2)}) %all-to-all-start.1) | async-done | bytes 3735584 | tf_op jit(solution)/shard_map/all_to_all | solution.py:402
  244.0 4.9 %all-to-all-start.2 = ((bf16[16,304,384]{2,1,0:T(8,128)(2,1)}), bf16[16,304,384]{2,1,0:T(8,128)(2,1)}, u32[]{:S(2)}, u32[]{:S(2)}) async-start(bf16[16,304,384]{2,1,0:T(8,128)(2,1)} %pad_maximum_fusion.1), calls=%async_computation.2 | async-start | bytes 7471104 | tf_op jit(solution)/shard_map/all_to_all | solution.py:402
  248.9 10.6 %shard_map.34 = bf16[16,2,48,768]{3,2,1,0:T(8,128)(2,1)S(1)} custom-call(bf16[16,304,384]{2,1,0:T(8,128)(2,1)} %all-to-all-done.1.refs_0_.refs_1_.refs_2_.refs_3_, bf16[16,304,384]{2,1,0:T(8,128)(2,1)} %all-to-all-done.1.refs_0_.refs_1_.refs_2_.refs_3_, bf16[16,304,384]{2,1,0:T(8,128)(2,1)} %all-to-all-done.1.refs_0_.refs_1_.refs_2_.refs_3_, ...), custom_call_target="tpu_custom_call" | custom-call | flops 7247757312 | bytes 4718592 | tf_op jit(solution)/shard_map/pallas_call | solution.py:135
  259.4 10.8 %shard_map.33 = bf16[16,2,48,768]{3,2,1,0:T(8,128)(2,1)S(1)} custom-call(bf16[16,304,384]{2,1,0:T(8,128)(2,1)} %all-to-all-done.1.refs_0_.refs_1_.refs_2_.refs_3_, bf16[16,304,384]{2,1,0:T(8,128)(2,1)} %all-to-all-done.1.refs_0_.refs_1_.refs_2_.refs_3_, bf16[16,304,384]{2,1,0:T(8,128)(2,1)} %all-to-all-done.1.refs_0_.refs_1_.refs_2_.refs_3_, ...), custom_call_target="tpu_custom_call" | custom-call | flops 7247757312 | bytes 4718592 | tf_op jit(solution)/shard_map/pallas_call | solution.py:135
  270.3 2.6 pad_maximum_fusion
  272.9 58.6 %all-to-all-done.2.x.re_ref.im_ref.mix_ref.tile_ref = bf16[16,304,384]{2,1,0:T(8,128)(2,1)} async-done(((bf16[16,304,384]{2,1,0:T(8,128)(2,1)}), bf16[16,304,384]{2,1,0:T(8,128)(2,1)}, u32[]{:S(2)}, u32[]{:S(2)}) %all-to-all-start.2) | async-done | bytes 3735584 | tf_op jit(solution)/shard_map/all_to_all | solution.py:402
  331.5 2.3 shard_map.35
  333.9 4.9 %copy.22 = bf16[16,2,2,48,768]{4,3,2,1,0:T(8,128)(2,1)} copy(bf16[16,2,2,48,768]{4,3,2,0,1:T(8,128)(2,1)} %pad_maximum_fusion) | data formatting | bytes 9437184 | tf_op jit(solution)/shard_map/optimization_barrier | solution.py:475
  338.8 5.0 %all-to-all-start.3 = ((bf16[16,2,2,48,768]{4,3,2,1,0:T(8,128)(2,1)}), bf16[16,2,2,48,768]{4,3,2,1,0:T(8,128)(2,1)}, u32[]{:S(2)}, u32[]{:S(2)}) async-start(bf16[16,2,2,48,768]{4,3,2,1,0:T(8,128)(2,1)} %copy.22), calls=%async_computation.3 | async-start | bytes 9437184 | tf_op jit(solution)/shard_map/all_to_all | solution.py:402
  343.8 0.4 collective-permute-start.7
  344.2 0.3 collective-permute-start.8
  344.5 1.5 collective-permute-start.9
  346.0 0.3 collective-permute-start.10
  346.3 1.4 collective-permute-start.11
  347.7 0.1 collective-permute-start.12
  347.7 25.8 %collective-permute-done.8.refs_2_ = bf16[48,1536]{1,0:T(8,128)(2,1)S(1)} collective-permute-done((bf16[48,1536]{1,0:T(8,128)(2,1)S(1)}, bf16[48,1536]{1,0:T(8,128)(2,1)S(1)}, u32[]{:S(2)}, u32[]{:S(2)}) %collective-permute-start.8) | collective-permute-done | bytes 147488 | tf_op jit(solution)/shard_map/ppermute | solution.py:395
  373.5 3.4 collective-permute-start.13
  376.9 0.1 copy.16
  377.0 0.1 copy.17
  377.2 48.1 %collective-permute-done.10.refs_4_ = bf16[48,1536]{1,0:T(8,128)(2,1)S(1)} collective-permute-done((bf16[48,1536]{1,0:T(8,128)(2,1)S(1)}, bf16[48,1536]{1,0:T(8,128)(2,1)S(1)}, u32[]{:S(2)}, u32[]{:S(2)}) %collective-permute-start.10) | collective-permute-done | bytes 147488 | tf_op jit(solution)/shard_map/ppermute | solution.py:395
  425.2 4.1 collective-permute-done.11.refs_5_
  429.4 1.3 collective-permute-done.12.refs_6_
  430.7 3.2 collective-permute-done.13.refs_7_
  433.8 6.4 %shard_map.36 = bf16[32,2,48,768]{3,2,1,0:T(8,128)(2,1)} custom-call(s32[2]{0:T(128)S(1)} %pad_add_fusion.where_ref, bf16[16,304,384]{2,1,0:T(8,128)(2,1)} %all-to-all-done.2.x.re_ref.im_ref.mix_ref.tile_ref, bf16[16,304,384]{2,1,0:T(8,128)(2,1)} %all-to-all-done.2.x.re_ref.im_ref.mix_ref.tile_ref, ...), custom_call_target="tpu_custom_call" | custom-call | bytes 11796480 | tf_op jit(solution)/shard_map/pallas_call | solution.py:368
  440.3 7.3 %all-to-all-done.3 = bf16[16,2,2,48,768]{4,3,2,1,0:T(8,128)(2,1)} async-done(((bf16[16,2,2,48,768]{4,3,2,1,0:T(8,128)(2,1)}), bf16[16,2,2,48,768]{4,3,2,1,0:T(8,128)(2,1)}, u32[]{:S(2)}, u32[]{:S(2)}) %all-to-all-start.3) | async-done | bytes 4718624 | tf_op jit(solution)/shard_map/all_to_all | solution.py:402
  447.6 18.9 %shard_map.37 = bf16[48,768,512]{2,1,0:T(8,128)(2,1)} custom-call(bf16[128,512]{1,0:T(8,128)(2,1)S(1)} %pad_maximum_fusion.2.table, bf16[64,48,768]{2,1,0:T(8,128)(2,1)} %bitcast.23, bf16[64,48,768]{2,1,0:T(8,128)(2,1)} %bitcast.12.refs_1_), custom_call_target="tpu_custom_call" | custom-call | flops 9663676416 | bytes 47185920 | tf_op jit(solution)/shard_map/pallas_call | solution.py:225
  (24 shorter events, 0.2 us)
Async XLA Ops:
  7.7 0.6 copy-start.5
  7.7 0.8 copy-start.3
  30.7 2.3 copy-start
  35.0 117.4 %all-to-all-start = ((bf16[16,2,2,48,768]{4,3,2,1,0:T(8,128)(2,1)}), bf16[16,2,2,48,768]{4,3,2,1,0:T(8,128)(2,1)}, u32[]{:S(2)}, u32[]{:S(2)}) async-start(bf16[16,2,2,48,768]{4,3,2,1,0:T(8,128)(2,1)} %bitcast.24), calls=%async_computation | async-start | bytes 9437184 | tf_op jit(solution)/shard_map/all_to_all | solution.py:402
  41.5 104.8 %all-gather.2.cloned.1.call-start = ((), (), s32[]{:S(2)}) async-start(), calls=%async_computation.4 | async-start | bytes 1253376 | tf_op jit(solution)/shard_map/all_gather | solution.py:445
  42.3 3.9 collective-permute-start
  42.7 23.3 %collective-permute-start.1 = (bf16[48,1536]{1,0:T(8,128)(2,1)S(1)}, bf16[48,1536]{1,0:T(8,128)(2,1)S(1)}, u32[]{:S(2)}, u32[]{:S(2)}) collective-permute-start(bf16[48,1536]{1,0:T(8,128)(2,1)S(1)} %get-tuple-element.58), channel_id=1, source_target_pairs={{0,2},{1,3},{2,0},{3,1},{4,6},{5,7},{6,4},{7,5},{8,10},{9,11},{10,... | collective-permute-start | bytes 442376 | tf_op jit(solution)/shard_map/ppermute | solution.py:395
  43.0 32.4 %collective-permute-start.2 = (bf16[48,1536]{1,0:T(8,128)(2,1)S(1)}, bf16[48,1536]{1,0:T(8,128)(2,1)S(1)}, u32[]{:S(2)}, u32[]{:S(2)}) collective-permute-start(bf16[48,1536]{1,0:T(8,128)(2,1)S(1)} %get-tuple-element.59), channel_id=1, source_target_pairs={{0,3},{1,2},{2,1},{3,0},{4,7},{5,6},{6,5},{7,4},{8,11},{9,10},{10,... | collective-permute-start | bytes 442376 | tf_op jit(solution)/shard_map/ppermute | solution.py:395
  44.5 85.4 %collective-permute-start.3 = (bf16[48,1536]{1,0:T(8,128)(2,1)S(1)}, bf16[48,1536]{1,0:T(8,128)(2,1)S(1)}, u32[]{:S(2)}, u32[]{:S(2)}) collective-permute-start(bf16[48,1536]{1,0:T(8,128)(2,1)S(1)} %get-tuple-element.60), channel_id=1, source_target_pairs={{0,4},{1,5},{2,6},{3,7},{4,0},{5,1},{6,2},{7,3},{8,12},{9,13},{10,... | collective-permute-start | bytes 442376 | tf_op jit(solution)/shard_map/ppermute | solution.py:395
  44.8 89.2 %collective-permute-start.4 = (bf16[48,1536]{1,0:T(8,128)(2,1)S(1)}, bf16[48,1536]{1,0:T(8,128)(2,1)S(1)}, u32[]{:S(2)}, u32[]{:S(2)}) collective-permute-start(bf16[48,1536]{1,0:T(8,128)(2,1)S(1)} %get-tuple-element.61), channel_id=1, source_target_pairs={{0,5},{1,4},{2,7},{3,6},{4,1},{5,0},{6,3},{7,2},{8,13},{9,12},{10,... | collective-permute-start | bytes 442376 | tf_op jit(solution)/shard_map/ppermute | solution.py:395
  46.2 89.2 %collective-permute-start.5 = (bf16[48,1536]{1,0:T(8,128)(2,1)S(1)}, bf16[48,1536]{1,0:T(8,128)(2,1)S(1)}, u32[]{:S(2)}, u32[]{:S(2)}) collective-permute-start(bf16[48,1536]{1,0:T(8,128)(2,1)S(1)} %get-tuple-element.62), channel_id=1, source_target_pairs={{0,6},{1,7},{2,4},{3,5},{4,2},{5,3},{6,0},{7,1},{8,14},{9,15},{10,... | collective-permute-start | bytes 442376 | tf_op jit(solution)/shard_map/ppermute | solution.py:395
  66.0 72.5 %collective-permute-start.6 = (bf16[48,1536]{1,0:T(8,128)(2,1)S(1)}, bf16[48,1536]{1,0:T(8,128)(2,1)S(1)}, u32[]{:S(2)}, u32[]{:S(2)}) collective-permute-start(bf16[48,1536]{1,0:T(8,128)(2,1)S(1)} %get-tuple-element.63), channel_id=1, source_target_pairs={{0,7},{1,6},{2,5},{3,4},{4,3},{5,2},{6,1},{7,0},{8,15},{9,14},{10,... | collective-permute-start | bytes 442376 | tf_op jit(solution)/shard_map/ppermute | solution.py:395
  144.5 1.8 copy-start.1
  146.3 15.0 %copy-start.2 = (bf16[768,768]{1,0:T(8,128)(2,1)S(1)}, bf16[768,768]{1,0:T(8,128)(2,1)}, u32[]{:S(2)}) copy-start(bf16[768,768]{1,0:T(8,128)(2,1)} %all-gather.2.cloned.1.call-done) | copy-start | bytes 3538948
  152.3 91.6 %all-to-all-start.1 = ((bf16[16,304,384]{2,1,0:T(8,128)(2,1)}), bf16[16,304,384]{2,1,0:T(8,128)(2,1)}, u32[]{:S(2)}, u32[]{:S(2)}) async-start(bf16[16,304,384]{2,1,0:T(8,128)(2,1)} %copy-done.1), calls=%async_computation.1 | async-start | bytes 7471104 | tf_op jit(solution)/shard_map/all_to_all | solution.py:402
  244.0 87.5 %all-to-all-start.2 = ((bf16[16,304,384]{2,1,0:T(8,128)(2,1)}), bf16[16,304,384]{2,1,0:T(8,128)(2,1)}, u32[]{:S(2)}, u32[]{:S(2)}) async-start(bf16[16,304,384]{2,1,0:T(8,128)(2,1)} %pad_maximum_fusion.1), calls=%async_computation.2 | async-start | bytes 7471104 | tf_op jit(solution)/shard_map/all_to_all | solution.py:402
  338.8 38.2 %copy-start.6 = (bf16[32,2,512]{2,0,1:T(8,128)(2,1)S(1)}, bf16[32,2,512]{2,0,1:T(8,128)(2,1)}, u32[]{:S(2)}) copy-start(bf16[32,2,512]{2,0,1:T(8,128)(2,1)} %copy-done.5) | copy-start | bytes 196612
  338.8 38.2 %copy-start.4 = (bf16[32,2,512]{2,0,1:T(8,128)(2,1)S(1)}, bf16[32,2,512]{2,0,1:T(8,128)(2,1)}, u32[]{:S(2)}) copy-start(bf16[32,2,512]{2,0,1:T(8,128)(2,1)} %copy-done.3) | copy-start | bytes 196612
  338.8 108.8 %all-to-all-start.3 = ((bf16[16,2,2,48,768]{4,3,2,1,0:T(8,128)(2,1)}), bf16[16,2,2,48,768]{4,3,2,1,0:T(8,128)(2,1)}, u32[]{:S(2)}, u32[]{:S(2)}) async-start(bf16[16,2,2,48,768]{4,3,2,1,0:T(8,128)(2,1)} %copy.22), calls=%async_computation.3 | async-start | bytes 9437184 | tf_op jit(solution)/shard_map/all_to_all | solution.py:402
  343.8 3.9 collective-permute-start.7
  344.2 29.3 %collective-permute-start.8 = (bf16[48,1536]{1,0:T(8,128)(2,1)S(1)}, bf16[48,1536]{1,0:T(8,128)(2,1)S(1)}, u32[]{:S(2)}, u32[]{:S(2)}) collective-permute-start(bf16[48,1536]{1,0:T(8,128)(2,1)S(1)} %get-tuple-element.78), channel_id=1, source_target_pairs={{0,2},{1,3},{2,0},{3,1},{4,6},{5,7},{6,4},{7,5},{8,10},{9,11},{10,... | collective-permute-start | bytes 442376 | tf_op jit(solution)/shard_map/ppermute | solution.py:395
  344.5 32.7 %collective-permute-start.9 = (bf16[48,1536]{1,0:T(8,128)(2,1)S(1)}, bf16[48,1536]{1,0:T(8,128)(2,1)S(1)}, u32[]{:S(2)}, u32[]{:S(2)}) collective-permute-start(bf16[48,1536]{1,0:T(8,128)(2,1)S(1)} %get-tuple-element.79), channel_id=1, source_target_pairs={{0,3},{1,2},{2,1},{3,0},{4,7},{5,6},{6,5},{7,4},{8,11},{9,10},{10,... | collective-permute-start | bytes 442376 | tf_op jit(solution)/shard_map/ppermute | solution.py:395
  346.0 79.3 %collective-permute-start.10 = (bf16[48,1536]{1,0:T(8,128)(2,1)S(1)}, bf16[48,1536]{1,0:T(8,128)(2,1)S(1)}, u32[]{:S(2)}, u32[]{:S(2)}) collective-permute-start(bf16[48,1536]{1,0:T(8,128)(2,1)S(1)} %get-tuple-element.80), channel_id=1, source_target_pairs={{0,4},{1,5},{2,6},{3,7},{4,0},{5,1},{6,2},{7,3},{8,12},{9,13},{10,... | collective-permute-start | bytes 442376 | tf_op jit(solution)/shard_map/ppermute | solution.py:395
  346.3 83.1 %collective-permute-start.11 = (bf16[48,1536]{1,0:T(8,128)(2,1)S(1)}, bf16[48,1536]{1,0:T(8,128)(2,1)S(1)}, u32[]{:S(2)}, u32[]{:S(2)}) collective-permute-start(bf16[48,1536]{1,0:T(8,128)(2,1)S(1)} %get-tuple-element.81), channel_id=1, source_target_pairs={{0,5},{1,4},{2,7},{3,6},{4,1},{5,0},{6,3},{7,2},{8,13},{9,12},{10,... | collective-permute-start | bytes 442376 | tf_op jit(solution)/shard_map/ppermute | solution.py:395
  347.7 83.0 %collective-permute-start.12 = (bf16[48,1536]{1,0:T(8,128)(2,1)S(1)}, bf16[48,1536]{1,0:T(8,128)(2,1)S(1)}, u32[]{:S(2)}, u32[]{:S(2)}) collective-permute-start(bf16[48,1536]{1,0:T(8,128)(2,1)S(1)} %get-tuple-element.82), channel_id=1, source_target_pairs={{0,6},{1,7},{2,4},{3,5},{4,2},{5,3},{6,0},{7,1},{8,14},{9,15},{10,... | collective-permute-start | bytes 442376 | tf_op jit(solution)/shard_map/ppermute | solution.py:395
  373.5 60.3 %collective-permute-start.13 = (bf16[48,1536]{1,0:T(8,128)(2,1)S(1)}, bf16[48,1536]{1,0:T(8,128)(2,1)S(1)}, u32[]{:S(2)}, u32[]{:S(2)}) collective-permute-start(bf16[48,1536]{1,0:T(8,128)(2,1)S(1)} %get-tuple-element.83), channel_id=1, source_target_pairs={{0,7},{1,6},{2,5},{3,4},{4,3},{5,2},{6,1},{7,0},{8,15},{9,14},{10,... | collective-permute-start | bytes 442376 | tf_op jit(solution)/shard_map/ppermute | solution.py:395
Sparse Core Ops, SparseCore 0:
  44.6 83.3 all-gather.1

commit v4 on v3

--- a/solution.py
+++ b/solution.py
@@ -46,6 +46,8 @@
 
 def chain_kernel(rows, slot_in, slot_out, packed_in, packed_out, *refs):
     count = 4 if packed_in else 1
+    if slot_in is None:
+        slot_in = pl.program_id(0)
     ins, ratio, out, (br, bi, fr, fi) = refs[:count], refs[count], refs[count + 1], refs[count + 2 :]
     order = br.shape[0]
     half = order // 2
@@ -67,9 +69,9 @@
             both = mix[h * (n // 2) : (h + 1) * (n // 2)].reshape(half, half).astype(f32)
             tr = jnp.where(mask, 0.0, both)
             br[pick, pick] = ((tr + tr.T) * ratio[pick, pick]).astype(b16)
-            line = jnp.sum(
-                extra[h * (n // 2) : (h + 1) * (n // 2), slot_in : slot_in + 1].astype(f32), axis=0
-            )
+            lines = extra[h * (n // 2) : (h + 1) * (n // 2)].astype(f32)
+            chosen = lax.broadcasted_iota(jnp.int32, (n // 2, TILE, half), 1) == slot_in
+            line = jnp.sum(jnp.sum(jnp.where(chosen, lines, 0.0), axis=0), axis=0, keepdims=True)
             ti = jnp.where(mask, both, 0.0)
             ti = ti + ti.T + jnp.where(diag, 2.0 * line, 0.0)
             bi[pick, pick] = (ti * ratio[pick, pick]).astype(b16)
@@ -112,8 +114,8 @@
             ).astype(b16)
             out[dst, 3 * rows :] = jnp.broadcast_to(tile[None], (n // 2, TILE, half))
     else:
-        out[:, 0] = fr[...].astype(b16).reshape(n, rows, order)
-        out[:, 1] = fi[...].astype(b16).reshape(n, rows, order)
+        out[:, 0, 0] = fr[...].astype(b16).reshape(n, rows, order)
+        out[:, 0, 1] = fi[...].astype(b16).reshape(n, rows, order)
 
 
 def chain(got, ratio, rows, order, slot_in, total_in, slot_out, packed_out):
@@ -149,6 +151,34 @@
             flops=16 * order**3, bytes_accessed=8 * order * order, transcendentals=0
         ),
     )(*args)
+
+
+def chain_group(got, ratio, rows, order, count):
+    n, half = order // rows, order // 2
+    specs = [
+        pl.BlockSpec((n, rows, half), functools.partial(lambda c, f: (0, 3 * f + c, 0), c))
+        for c in range(3)
+    ]
+    last = 3 * rows * count // TILE
+    specs.append(pl.BlockSpec((n, TILE, half), lambda f: (0, last, 0)))
+    specs.append(pl.BlockSpec((order, order), lambda f: (0, 0)))
+    return pl.pallas_call(
+        functools.partial(chain_kernel, rows, None, 0, True, False),
+        out_shape=jax.ShapeDtypeStruct((n, count, 2, rows, order), jnp.bfloat16),
+        grid=(count,),
+        in_specs=specs,
+        out_specs=pl.BlockSpec((n, 1, 2, rows, order), lambda f: (0, f, 0, 0, 0)),
+        scratch_shapes=[
+            pltpu.VMEM((order, order), jnp.bfloat16),
+            pltpu.VMEM((order, order), jnp.bfloat16),
+            pltpu.VMEM((order, order), jnp.float32),
+            pltpu.VMEM((order, order), jnp.float32),
+        ],
+        compiler_params=pltpu.CompilerParams(vmem_limit_bytes=48 * 1024 * 1024),
+        cost_estimate=pl.CostEstimate(
+            flops=16 * count * order**3, bytes_accessed=8 * count * order * order, transcendentals=0
+        ),
+    )(*[got] * 4, ratio)
 
 
 def dft_kernel(first, table, weight, traces, head, tail, turn):
@@ -469,8 +499,7 @@
     back = jnp.concatenate([part[:, : 3 * rows] for part in parts] + [tile], 1)
     back, got = lax.optimization_barrier((back, got))
     back = a2a(back)
-    parts = [chain(got, ratio, rows, order, f, rest, 0, False) for f in range(rest)]
-    parts = jnp.stack(parts, 1)
+    parts = chain_group(got, ratio, rows, order, rest)
     gifts = give(back, where, rows, group, 0, lead, False)
     parts, gifts = lax.optimization_barrier((parts, gifts))
     last = a2a(parts)

time: 483 us -> 478 us (0.990)
  local copies, waits for them, and re-layouts: 13.3 us -> 8.11 us
    pallas_call x4 -> x2, Pallas kernels: 41.9 us -> 20.6 us  [chain(): pl.pallas_call(functools.partial(chain_kernel, rows, slot_in, slot_out, p...]
    pallas_call x0 -> x1, Pallas kernels: none -> 21.2 us  [chain_group(): pl.pallas_call(functools.partial(chain_kernel, rows, None, 0, True, False...]
    optimization_barrier x1 -> x0, local copies, waits for them, and re-layouts: 4.91 us -> none  [pipelined(): parts, gifts = lax.optimization_barrier((parts, gifts))]
  transfers between devices with their start and end apart: 19 -> 19, of which waited for: 15 -> 15; matrix products, arithmetic and copies ran while one was open for 2% -> 2% of each run, Pallas kernels for 11% -> 12%
where the time goes in v4:
time: 478 us; the launch traced here: 469 us
  waiting for transfers between devices  296 us (62%)
  Pallas kernels  97.9 us (20%)
  starting transfers between devices  46.3 us (10%)
  between operations  14.1 us (3%)
  local copies, waits for them, and re-layouts  8.11 us (2%)
  other arithmetic  6.9 us (1%)
    ppermute x14, waiting for transfers between devices, swap(): lax.ppermute(piece, 'tile', [(i, i ^ m) for i in range(n)])  165 us
    all_to_all x4, waiting for transfers between devices, a2a(): return lax.all_to_all(x, 'tile', split_axis=0, concat_axis=0, tiled=True)  130 us
    all_to_all x4, starting transfers between devices, a2a(): return lax.all_to_all(x, 'tile', split_axis=0, concat_axis=0, tiled=True)  25.9 us
    pallas_call x1, Pallas kernels, chain_group(): pl.pallas_call(functools.partial(chain_kernel, rows, None, 0, True, False...  21.2 us
    pallas_call x2, Pallas kernels, chain(): pl.pallas_call(functools.partial(chain_kernel, rows, slot_in, slot_out, p...  20.6 us
    pallas_call x1, Pallas kernels, dft(): pl.pallas_call(functools.partial(dft_kernel, first), out_shape=[jax.Shape...  20.5 us
    ppermute x14, starting transfers between devices, swap(): lax.ppermute(piece, 'tile', [(i, i ^ m) for i in range(n)])  20.4 us
    pallas_call x1, Pallas kernels, idft(): pl.pallas_call(functools.partial(idft_kernel, len(pieces)), out_shape=jax...  18.9 us
  transfers between devices with their start and end apart: 19, of which 15 were waited for; matrix products, arithmetic and copies ran while one was open for 2% of the time, Pallas kernels for 12%

profile of v4, /device:TPU:15, one launch (start us, length us, event | category | flops | bytes accessed | tf_op | source)
XLA Modules:
  0.0 469.2 jit_solution(758107927659805914)
XLA Ops:
  6.5 0.6 fusion.7
  7.1 0.6 multiply_convert_fusion.1
  7.7 0.6 copy-done.5
  8.3 0.1 copy.21
  8.4 0.1 copy.17
  8.6 1.6 fusion.9
  10.1 0.1 pad_add_fusion.where_ref
  10.2 20.5 %shard_map.28 = (bf16[64,48,768]{2,1,0:T(8,128)(2,1)}, bf16[64,48,768]{2,1,0:T(8,128)(2,1)}) custom-call(bf16[128,512]{1,0:T(8,128)(2,1)S(1)} %pad_maximum_fusion.2.table, f32[48,768]{1,0:T(8,128)S(1)} %get-tuple-element.86.weight, bf16[48,768,512]{2,1,0:T(8,128)(2,1)} %traces.1), custom_call_target="tpu_custom_call" | custom-call | flops 9663676416 | bytes 47185920 | tf_op jit(solution)/shard_map/pallas_call | solution.py:205
  30.7 2.3 copy-done
  33.0 1.9 shard_map.29
  35.0 6.6 %all-to-all-start = ((bf16[16,2,2,48,768]{4,3,2,1,0:T(8,128)(2,1)}), bf16[16,2,2,48,768]{4,3,2,1,0:T(8,128)(2,1)}, u32[]{:S(2)}, u32[]{:S(2)}) async-start(bf16[16,2,2,48,768]{4,3,2,1,0:T(8,128)(2,1)} %bitcast.20), calls=%async_computation | async-start | bytes 9437184 | tf_op jit(solution)/shard_map/all_to_all | solution.py:432
  41.5 0.0 all-gather.2.cloned.1.call-start
  41.6 0.7 all-gather.2.cloned.1.call-update
  42.3 0.4 collective-permute-start
  42.7 0.3 collective-permute-start.1
  43.0 1.5 collective-permute-start.2
  44.5 0.3 collective-permute-start.3
  44.8 1.4 collective-permute-start.4
  46.2 0.0 collective-permute-done.refs_1_
  46.2 0.1 collective-permute-start.5
  46.2 19.8 %collective-permute-done.1.refs_2_ = bf16[48,1536]{1,0:T(8,128)(2,1)S(1)} collective-permute-done((bf16[48,1536]{1,0:T(8,128)(2,1)S(1)}, bf16[48,1536]{1,0:T(8,128)(2,1)S(1)}, u32[]{:S(2)}, u32[]{:S(2)}) %collective-permute-start.1) | collective-permute-done | bytes 147488 | tf_op jit(solution)/shard_map/ppermute | solution.py:425
  66.0 9.1 %collective-permute-start.6 = (bf16[48,1536]{1,0:T(8,128)(2,1)S(1)}, bf16[48,1536]{1,0:T(8,128)(2,1)S(1)}, u32[]{:S(2)}, u32[]{:S(2)}) collective-permute-start(bf16[48,1536]{1,0:T(8,128)(2,1)S(1)} %get-tuple-element.63), channel_id=1, source_target_pairs={{0,7},{1,6},{2,5},{3,4},{4,3},{5,2},{6,1},{7,0},{8,15},{9,14},{10,... | collective-permute-start | bytes 442376 | tf_op jit(solution)/shard_map/ppermute | solution.py:425
  75.1 0.3 collective-permute-done.2.refs_3_
  75.4 54.5 %collective-permute-done.3.refs_4_ = bf16[48,1536]{1,0:T(8,128)(2,1)S(1)} collective-permute-done((bf16[48,1536]{1,0:T(8,128)(2,1)S(1)}, bf16[48,1536]{1,0:T(8,128)(2,1)S(1)}, u32[]{:S(2)}, u32[]{:S(2)}) %collective-permute-start.3) | collective-permute-done | bytes 147488 | tf_op jit(solution)/shard_map/ppermute | solution.py:425
  129.9 4.1 collective-permute-done.4.refs_5_
  134.0 1.4 collective-permute-done.5.refs_6_
  135.4 3.2 collective-permute-done.6.refs_7_
  138.5 6.0 %shard_map.30 = bf16[16,304,384]{2,1,0:T(8,128)(2,1)S(1)} custom-call(s32[2]{0:T(128)S(1)} %pad_add_fusion.where_ref, bf16[2,16,2,48,768]{4,3,2,1,0:T(8,128)(2,1)} %bitcast.17, bf16[48,1536]{1,0:T(8,128)(2,1)S(1)} %get-tuple-element.56.refs_0_, bf16[48,1536]{1,0:T(8,128)(2,1)S(1)} %collective-permute-done.refs_1_, ...), custom_call_target="tpu_custom_call" | custom-call | bytes 11796480 | tf_op jit(solution)/shard_map/pallas_call | solution.py:353
  144.5 1.8 copy-done.1
  146.3 6.0 %all-to-all-done.refs_0_ = bf16[16,2,2,48,768]{4,3,2,1,0:T(8,128)(2,1)} async-done(((bf16[16,2,2,48,768]{4,3,2,1,0:T(8,128)(2,1)}), bf16[16,2,2,48,768]{4,3,2,1,0:T(8,128)(2,1)}, u32[]{:S(2)}, u32[]{:S(2)}) %all-to-all-start) | async-done | bytes 4718624 | tf_op jit(solution)/shard_map/all_to_all | solution.py:432
  152.3 9.0 %all-to-all-start.1 = ((bf16[16,304,384]{2,1,0:T(8,128)(2,1)}), bf16[16,304,384]{2,1,0:T(8,128)(2,1)}, u32[]{:S(2)}, u32[]{:S(2)}) async-start(bf16[16,304,384]{2,1,0:T(8,128)(2,1)} %copy-done.1), calls=%async_computation.1 | async-start | bytes 7471104 | tf_op jit(solution)/shard_map/all_to_all | solution.py:432
  161.3 0.6 copy.18
  162.0 1.9 copy.19
  163.9 2.1 fusion.refs_1_.refs_4_
  166.0 10.2 %shard_map.31 = bf16[16,160,384]{2,1,0:T(8,128)(2,1)S(1)} custom-call(bf16[16,2,2,48,768]{4,3,2,1,0:T(8,128)(2,1)} %all-to-all-done.refs_0_, f32[768,768]{1,0:T(8,128)S(1)} %fusion.refs_1_.refs_4_), custom_call_target="tpu_custom_call" | custom-call | flops 7247757312 | bytes 4718592 | tf_op jit(solution)/shard_map/pallas_call | solution.py:137
  176.2 0.2 slice.36
  176.4 10.4 %shard_map.32 = bf16[16,160,384]{2,1,0:T(8,128)(2,1)S(1)} custom-call(bf16[16,2,2,48,768]{4,3,2,1,0:T(8,128)(2,1)} %all-to-all-done.refs_0_, f32[768,768]{1,0:T(8,128)S(1)} %fusion.refs_1_.refs_4_), custom_call_target="tpu_custom_call" | custom-call | flops 7247757312 | bytes 4718592 | tf_op jit(solution)/shard_map/pallas_call | solution.py:137
  186.8 0.2 slice.37
  187.0 2.0 pad_maximum_fusion
  189.0 55.0 %all-to-all-done.1.refs_0_.refs_1_.refs_2_.refs_3_ = bf16[16,304,384]{2,1,0:T(8,128)(2,1)} async-done(((bf16[16,304,384]{2,1,0:T(8,128)(2,1)}), bf16[16,304,384]{2,1,0:T(8,128)(2,1)}, u32[]{:S(2)}, u32[]{:S(2)}) %all-to-all-start.1) | async-done | bytes 3735584 | tf_op jit(solution)/shard_map/all_to_all | solution.py:432
  244.0 4.9 %all-to-all-start.2 = ((bf16[16,304,384]{2,1,0:T(8,128)(2,1)}), bf16[16,304,384]{2,1,0:T(8,128)(2,1)}, u32[]{:S(2)}, u32[]{:S(2)}) async-start(bf16[16,304,384]{2,1,0:T(8,128)(2,1)} %pad_maximum_fusion), calls=%async_computation.2 | async-start | bytes 7471104 | tf_op jit(solution)/shard_map/all_to_all | solution.py:432
  248.9 21.2 %shard_map.33 = bf16[16,2,2,48,768]{4,3,2,1,0:T(8,128)(2,1)} custom-call(bf16[16,304,384]{2,1,0:T(8,128)(2,1)} %all-to-all-done.1.refs_0_.refs_1_.refs_2_.refs_3_, bf16[16,304,384]{2,1,0:T(8,128)(2,1)} %all-to-all-done.1.refs_0_.refs_1_.refs_2_.refs_3_, bf16[16,304,384]{2,1,0:T(8,128)(2,1)} %all-to-all-done.1.refs_0_.refs_1_.refs_2_.refs_3_, ...), custom_call_target="tpu_custom_call" | custom-call | flops 14495514624 | bytes 9437184 | tf_op jit(solution)/shard_map/pallas_call | solution.py:165
  270.1 61.4 %all-to-all-done.2.x.re_ref.im_ref.mix_ref.tile_ref = bf16[16,304,384]{2,1,0:T(8,128)(2,1)} async-done(((bf16[16,304,384]{2,1,0:T(8,128)(2,1)}), bf16[16,304,384]{2,1,0:T(8,128)(2,1)}, u32[]{:S(2)}, u32[]{:S(2)}) %all-to-all-start.2) | async-done | bytes 3735584 | tf_op jit(solution)/shard_map/all_to_all | solution.py:432
  331.5 2.3 shard_map.34
  333.9 5.4 %all-to-all-start.3 = ((bf16[16,2,2,48,768]{4,3,2,1,0:T(8,128)(2,1)}), bf16[16,2,2,48,768]{4,3,2,1,0:T(8,128)(2,1)}, u32[]{:S(2)}, u32[]{:S(2)}) async-start(bf16[16,2,2,48,768]{4,3,2,1,0:T(8,128)(2,1)} %shard_map.33), calls=%async_computation.3 | async-start | bytes 9437184 | tf_op jit(solution)/shard_map/all_to_all | solution.py:432
  339.3 0.4 collective-permute-start.7
  339.8 0.3 collective-permute-start.8
  340.0 1.5 collective-permute-start.9
  341.6 0.3 collective-permute-start.10
  341.8 1.4 collective-permute-start.11
  343.3 0.0 collective-permute-done.7.refs_1_
  343.3 0.1 collective-permute-start.12
  343.3 25.6 %collective-permute-done.8.refs_2_ = bf16[48,1536]{1,0:T(8,128)(2,1)S(1)} collective-permute-done((bf16[48,1536]{1,0:T(8,128)(2,1)S(1)}, bf16[48,1536]{1,0:T(8,128)(2,1)S(1)}, u32[]{:S(2)}, u32[]{:S(2)}) %collective-permute-start.8) | collective-permute-done | bytes 147488 | tf_op jit(solution)/shard_map/ppermute | solution.py:425
  368.9 3.4 collective-permute-start.13
  372.3 0.1 copy.14
  372.4 0.1 copy.15
  372.6 0.0 collective-permute-done.9.refs_3_
  372.6 48.0 %collective-permute-done.10.refs_4_ = bf16[48,1536]{1,0:T(8,128)(2,1)S(1)} collective-permute-done((bf16[48,1536]{1,0:T(8,128)(2,1)S(1)}, bf16[48,1536]{1,0:T(8,128)(2,1)S(1)}, u32[]{:S(2)}, u32[]{:S(2)}) %collective-permute-start.10) | collective-permute-done | bytes 147488 | tf_op jit(solution)/shard_map/ppermute | solution.py:425
  420.6 4.1 collective-permute-done.11.refs_5_
  424.7 1.3 collective-permute-done.12.refs_6_
  426.0 3.2 collective-permute-done.13.refs_7_
  429.2 6.5 %shard_map.35 = bf16[32,2,48,768]{3,2,1,0:T(8,128)(2,1)} custom-call(s32[2]{0:T(128)S(1)} %pad_add_fusion.where_ref, bf16[16,304,384]{2,1,0:T(8,128)(2,1)} %all-to-all-done.2.x.re_ref.im_ref.mix_ref.tile_ref, bf16[16,304,384]{2,1,0:T(8,128)(2,1)} %all-to-all-done.2.x.re_ref.im_ref.mix_ref.tile_ref, ...), custom_call_target="tpu_custom_call" | custom-call | bytes 11796480 | tf_op jit(solution)/shard_map/pallas_call | solution.py:398
  435.7 7.3 %all-to-all-done.3 = bf16[16,2,2,48,768]{4,3,2,1,0:T(8,128)(2,1)} async-done(((bf16[16,2,2,48,768]{4,3,2,1,0:T(8,128)(2,1)}), bf16[16,2,2,48,768]{4,3,2,1,0:T(8,128)(2,1)}, u32[]{:S(2)}, u32[]{:S(2)}) %all-to-all-start.3) | async-done | bytes 4718624 | tf_op jit(solution)/shard_map/all_to_all | solution.py:432
  443.0 18.9 %shard_map.36 = bf16[48,768,512]{2,1,0:T(8,128)(2,1)} custom-call(bf16[128,512]{1,0:T(8,128)(2,1)S(1)} %pad_maximum_fusion.1.table, bf16[64,48,768]{2,1,0:T(8,128)(2,1)} %bitcast.19, bf16[64,48,768]{2,1,0:T(8,128)(2,1)} %bitcast.10.refs_1_), custom_call_target="tpu_custom_call" | custom-call | flops 9663676416 | bytes 47185920 | tf_op jit(solution)/shard_map/pallas_call | solution.py:255
  (21 shorter events, 0.2 us)
Async XLA Ops:
  7.7 0.6 copy-start.5
  7.7 0.8 copy-start.3
  30.7 2.3 copy-start
  35.0 117.4 %all-to-all-start = ((bf16[16,2,2,48,768]{4,3,2,1,0:T(8,128)(2,1)}), bf16[16,2,2,48,768]{4,3,2,1,0:T(8,128)(2,1)}, u32[]{:S(2)}, u32[]{:S(2)}) async-start(bf16[16,2,2,48,768]{4,3,2,1,0:T(8,128)(2,1)} %bitcast.20), calls=%async_computation | async-start | bytes 9437184 | tf_op jit(solution)/shard_map/all_to_all | solution.py:432
  41.5 104.8 %all-gather.2.cloned.1.call-start = ((), (), s32[]{:S(2)}) async-start(), calls=%async_computation.4 | async-start | bytes 1253376 | tf_op jit(solution)/shard_map/all_gather | solution.py:475
  42.3 3.9 collective-permute-start
  42.7 23.3 %collective-permute-start.1 = (bf16[48,1536]{1,0:T(8,128)(2,1)S(1)}, bf16[48,1536]{1,0:T(8,128)(2,1)S(1)}, u32[]{:S(2)}, u32[]{:S(2)}) collective-permute-start(bf16[48,1536]{1,0:T(8,128)(2,1)S(1)} %get-tuple-element.58), channel_id=1, source_target_pairs={{0,2},{1,3},{2,0},{3,1},{4,6},{5,7},{6,4},{7,5},{8,10},{9,11},{10,... | collective-permute-start | bytes 442376 | tf_op jit(solution)/shard_map/ppermute | solution.py:425
  43.0 32.4 %collective-permute-start.2 = (bf16[48,1536]{1,0:T(8,128)(2,1)S(1)}, bf16[48,1536]{1,0:T(8,128)(2,1)S(1)}, u32[]{:S(2)}, u32[]{:S(2)}) collective-permute-start(bf16[48,1536]{1,0:T(8,128)(2,1)S(1)} %get-tuple-element.59), channel_id=1, source_target_pairs={{0,3},{1,2},{2,1},{3,0},{4,7},{5,6},{6,5},{7,4},{8,11},{9,10},{10,... | collective-permute-start | bytes 442376 | tf_op jit(solution)/shard_map/ppermute | solution.py:425
  44.5 85.4 %collective-permute-start.3 = (bf16[48,1536]{1,0:T(8,128)(2,1)S(1)}, bf16[48,1536]{1,0:T(8,128)(2,1)S(1)}, u32[]{:S(2)}, u32[]{:S(2)}) collective-permute-start(bf16[48,1536]{1,0:T(8,128)(2,1)S(1)} %get-tuple-element.60), channel_id=1, source_target_pairs={{0,4},{1,5},{2,6},{3,7},{4,0},{5,1},{6,2},{7,3},{8,12},{9,13},{10,... | collective-permute-start | bytes 442376 | tf_op jit(solution)/shard_map/ppermute | solution.py:425
  44.8 89.2 %collective-permute-start.4 = (bf16[48,1536]{1,0:T(8,128)(2,1)S(1)}, bf16[48,1536]{1,0:T(8,128)(2,1)S(1)}, u32[]{:S(2)}, u32[]{:S(2)}) collective-permute-start(bf16[48,1536]{1,0:T(8,128)(2,1)S(1)} %get-tuple-element.61), channel_id=1, source_target_pairs={{0,5},{1,4},{2,7},{3,6},{4,1},{5,0},{6,3},{7,2},{8,13},{9,12},{10,... | collective-permute-start | bytes 442376 | tf_op jit(solution)/shard_map/ppermute | solution.py:425
  46.2 89.2 %collective-permute-start.5 = (bf16[48,1536]{1,0:T(8,128)(2,1)S(1)}, bf16[48,1536]{1,0:T(8,128)(2,1)S(1)}, u32[]{:S(2)}, u32[]{:S(2)}) collective-permute-start(bf16[48,1536]{1,0:T(8,128)(2,1)S(1)} %get-tuple-element.62), channel_id=1, source_target_pairs={{0,6},{1,7},{2,4},{3,5},{4,2},{5,3},{6,0},{7,1},{8,14},{9,15},{10,... | collective-permute-start | bytes 442376 | tf_op jit(solution)/shard_map/ppermute | solution.py:425
  66.0 72.5 %collective-permute-start.6 = (bf16[48,1536]{1,0:T(8,128)(2,1)S(1)}, bf16[48,1536]{1,0:T(8,128)(2,1)S(1)}, u32[]{:S(2)}, u32[]{:S(2)}) collective-permute-start(bf16[48,1536]{1,0:T(8,128)(2,1)S(1)} %get-tuple-element.63), channel_id=1, source_target_pairs={{0,7},{1,6},{2,5},{3,4},{4,3},{5,2},{6,1},{7,0},{8,15},{9,14},{10,... | collective-permute-start | bytes 442376 | tf_op jit(solution)/shard_map/ppermute | solution.py:425
  144.5 1.8 copy-start.1
  146.3 15.0 %copy-start.2 = (bf16[768,768]{1,0:T(8,128)(2,1)S(1)}, bf16[768,768]{1,0:T(8,128)(2,1)}, u32[]{:S(2)}) copy-start(bf16[768,768]{1,0:T(8,128)(2,1)} %all-gather.2.cloned.1.call-done) | copy-start | bytes 3538948
  152.3 91.6 %all-to-all-start.1 = ((bf16[16,304,384]{2,1,0:T(8,128)(2,1)}), bf16[16,304,384]{2,1,0:T(8,128)(2,1)}, u32[]{:S(2)}, u32[]{:S(2)}) async-start(bf16[16,304,384]{2,1,0:T(8,128)(2,1)} %copy-done.1), calls=%async_computation.1 | async-start | bytes 7471104 | tf_op jit(solution)/shard_map/all_to_all | solution.py:432
  244.0 87.5 %all-to-all-start.2 = ((bf16[16,304,384]{2,1,0:T(8,128)(2,1)}), bf16[16,304,384]{2,1,0:T(8,128)(2,1)}, u32[]{:S(2)}, u32[]{:S(2)}) async-start(bf16[16,304,384]{2,1,0:T(8,128)(2,1)} %pad_maximum_fusion), calls=%async_computation.2 | async-start | bytes 7471104 | tf_op jit(solution)/shard_map/all_to_all | solution.py:432
  333.9 38.5 %copy-start.6 = (bf16[32,2,512]{2,0,1:T(8,128)(2,1)S(1)}, bf16[32,2,512]{2,0,1:T(8,128)(2,1)}, u32[]{:S(2)}) copy-start(bf16[32,2,512]{2,0,1:T(8,128)(2,1)} %copy-done.5) | copy-start | bytes 196612
  333.9 38.5 %copy-start.4 = (bf16[32,2,512]{2,0,1:T(8,128)(2,1)S(1)}, bf16[32,2,512]{2,0,1:T(8,128)(2,1)}, u32[]{:S(2)}) copy-start(bf16[32,2,512]{2,0,1:T(8,128)(2,1)} %copy-done.3) | copy-start | bytes 196612
  333.9 109.1 %all-to-all-start.3 = ((bf16[16,2,2,48,768]{4,3,2,1,0:T(8,128)(2,1)}), bf16[16,2,2,48,768]{4,3,2,1,0:T(8,128)(2,1)}, u32[]{:S(2)}, u32[]{:S(2)}) async-start(bf16[16,2,2,48,768]{4,3,2,1,0:T(8,128)(2,1)} %shard_map.33), calls=%async_computation.3 | async-start | bytes 9437184 | tf_op jit(solution)/shard_map/all_to_all | solution.py:432
  339.3 3.9 collective-permute-start.7
  339.8 29.2 %collective-permute-start.8 = (bf16[48,1536]{1,0:T(8,128)(2,1)S(1)}, bf16[48,1536]{1,0:T(8,128)(2,1)S(1)}, u32[]{:S(2)}, u32[]{:S(2)}) collective-permute-start(bf16[48,1536]{1,0:T(8,128)(2,1)S(1)} %get-tuple-element.78), channel_id=1, source_target_pairs={{0,2},{1,3},{2,0},{3,1},{4,6},{5,7},{6,4},{7,5},{8,10},{9,11},{10,... | collective-permute-start | bytes 442376 | tf_op jit(solution)/shard_map/ppermute | solution.py:425
  340.0 32.5 %collective-permute-start.9 = (bf16[48,1536]{1,0:T(8,128)(2,1)S(1)}, bf16[48,1536]{1,0:T(8,128)(2,1)S(1)}, u32[]{:S(2)}, u32[]{:S(2)}) collective-permute-start(bf16[48,1536]{1,0:T(8,128)(2,1)S(1)} %get-tuple-element.79), channel_id=1, source_target_pairs={{0,3},{1,2},{2,1},{3,0},{4,7},{5,6},{6,5},{7,4},{8,11},{9,10},{10,... | collective-permute-start | bytes 442376 | tf_op jit(solution)/shard_map/ppermute | solution.py:425
  341.6 79.0 %collective-permute-start.10 = (bf16[48,1536]{1,0:T(8,128)(2,1)S(1)}, bf16[48,1536]{1,0:T(8,128)(2,1)S(1)}, u32[]{:S(2)}, u32[]{:S(2)}) collective-permute-start(bf16[48,1536]{1,0:T(8,128)(2,1)S(1)} %get-tuple-element.80), channel_id=1, source_target_pairs={{0,4},{1,5},{2,6},{3,7},{4,0},{5,1},{6,2},{7,3},{8,12},{9,13},{10,... | collective-permute-start | bytes 442376 | tf_op jit(solution)/shard_map/ppermute | solution.py:425
  341.8 82.9 %collective-permute-start.11 = (bf16[48,1536]{1,0:T(8,128)(2,1)S(1)}, bf16[48,1536]{1,0:T(8,128)(2,1)S(1)}, u32[]{:S(2)}, u32[]{:S(2)}) collective-permute-start(bf16[48,1536]{1,0:T(8,128)(2,1)S(1)} %get-tuple-element.81), channel_id=1, source_target_pairs={{0,5},{1,4},{2,7},{3,6},{4,1},{5,0},{6,3},{7,2},{8,13},{9,12},{10,... | collective-permute-start | bytes 442376 | tf_op jit(solution)/shard_map/ppermute | solution.py:425
  343.3 82.8 %collective-permute-start.12 = (bf16[48,1536]{1,0:T(8,128)(2,1)S(1)}, bf16[48,1536]{1,0:T(8,128)(2,1)S(1)}, u32[]{:S(2)}, u32[]{:S(2)}) collective-permute-start(bf16[48,1536]{1,0:T(8,128)(2,1)S(1)} %get-tuple-element.82), channel_id=1, source_target_pairs={{0,6},{1,7},{2,4},{3,5},{4,2},{5,3},{6,0},{7,1},{8,14},{9,15},{10,... | collective-permute-start | bytes 442376 | tf_op jit(solution)/shard_map/ppermute | solution.py:425
  368.9 60.3 %collective-permute-start.13 = (bf16[48,1536]{1,0:T(8,128)(2,1)S(1)}, bf16[48,1536]{1,0:T(8,128)(2,1)S(1)}, u32[]{:S(2)}, u32[]{:S(2)}) collective-permute-start(bf16[48,1536]{1,0:T(8,128)(2,1)S(1)} %get-tuple-element.83), channel_id=1, source_target_pairs={{0,7},{1,6},{2,5},{3,4},{4,3},{5,2},{6,1},{7,0},{8,15},{9,14},{10,... | collective-permute-start | bytes 442376 | tf_op jit(solution)/shard_map/ppermute | solution.py:425
Sparse Core Ops, SparseCore 0:
  44.6 83.3 all-gather.1
